TPU v7x, 512 devices: a whole 4x8x8 slice. The times are simulated.
512 devices in a mesh: grp: 16 (over x, z_hi, core), ctx: 32 (over y, z_lo).
Axes of the slice: x: 4, y: 8, z: 8 (z_hi: 2, z_lo: 4; z = z_hi * 4 + z_lo), core: 2. Of those that a mesh axis runs over, the one named last changes fastest.
Arguments:
- queries: bfloat16 [32768, 4096], P(('grp', 'ctx')), may hold values from -200 to 200
- key_rows: bfloat16 [32768, 512], P(('grp', 'ctx')), may hold values from -10 to 10
- value_rows: bfloat16 [32768, 512], P(('grp', 'ctx')), may hold values from -6 to 6
- doc_ids: int32 [16, 2048], P('grp', 'ctx'), may hold values from 0 to 5, never falling along the last dimension, each value on 1 to 1024 neighbouring positions
Outputs:
- attended: bfloat16 [32768, 4096], P(('grp', 'ctx'))
- log_totals: float32 [32, 32768], P(None, ('grp', 'ctx'))
Inputs may be any that keep to these rules, and one draw needn't show every extreme that they name: `doc_ids`: nondecreasing along each group's tokens; every prompt has 1 to 1024 tokens and one has exactly 1024.
All inputs are finite; a program needn't handle non-finite values.
Results may differ from a plain program's by a relative error of at most 0.0065.
Values may be sent and summed in bfloat16 or wider, within the bound.
No kernel may reach another device: no remote copies, remote signals or barrier semaphores. Data moves between devices by JAX's collectives and lax.ppermute only.
A program may use at most 64 MiB of HBM per device.

v0:
```python
import jax
import jax.numpy as jnp
from jax import lax
from jax.sharding import PartitionSpec as P

QH = 32
KVH = 4
DH = 128


def partner(block, axis, bit):
    count = lax.axis_size(axis)
    route = []
    for low in range(count):
        high = low | 1 << bit
        if high != low and high < count:
            route += [(low, high), (high, low)]
    return lax.ppermute(block, axis, route)


def make_update(query, positions, doc_row):
    head_count = query.shape[1]
    score_scale = 1.0 / DH**0.5
    last_pos = positions[-1]
    first_doc = doc_row[0]

    def update(carries, key_piece, value_piece, doc_piece, offset):
        length = key_piece.shape[0]
        key_heads = key_piece.reshape(length, head_count, DH)
        value_heads = value_piece.reshape(length, head_count, DH)

        def compute(current):
            row_max, denominator, numerator = current
            scores = (
                jnp.einsum("tkgd,pkd->kgtp", query, key_heads, preferred_element_type=jnp.float32)
                * score_scale
            )
            key_pos = jnp.arange(length, dtype=jnp.int32)
            allowed = (key_pos[None, :] <= positions[:, None]) & (
                doc_piece[None, :] == doc_row[:, None]
            )
            masked = jnp.where(allowed, scores, -1e30)
            new_max = jnp.maximum(row_max, jnp.max(masked, axis=-1))
            weights = jnp.where(allowed, jnp.exp(scores - new_max[..., None]), 0.0)
            denominator = jnp.sum(weights, axis=-1)
            product = jnp.einsum(
                "kgtp,pkd->kgtd",
                weights.astype(jnp.bfloat16),
                value_heads,
                preferred_element_type=jnp.float32,
            )
            numerator = product
            return (new_max, denominator, numerator)

        def unchanged(current):
            return current

        needed = (offset <= last_pos) & (jnp.max(doc_piece) >= first_doc)
        return lax.cond(needed, compute, unchanged, carries)

    return update


def initial(query):
    shape = (query.shape[1], query.shape[2], query.shape[0])
    return (
        jnp.full(shape, -1e30, jnp.float32),
        jnp.zeros(shape, jnp.float32),
        jnp.zeros(shape + (DH,), jnp.float32),
    )


def finish(carries):
    row_max, denominator, numerator = carries
    attended = (numerator / denominator[..., None]).astype(jnp.bfloat16)
    attended = jnp.transpose(attended, (2, 0, 1, 3))
    log_totals = (row_max + jnp.log(denominator)).reshape(-1, row_max.shape[2])
    return (attended, log_totals)


def per_device(queries, key_rows, value_rows, doc_ids):
    row_count = queries.shape[0]
    ratio = QH // KVH
    doc_row = doc_ids[0]
    positions = lax.axis_index("ctx") * row_count + jnp.arange(row_count, dtype=jnp.int32)
    query = queries.reshape(row_count, KVH, ratio, DH)
    half_heads = KVH // 2
    group_count = lax.axis_size("grp")
    pair_bit = group_count.bit_length() - 2
    upper_half = lax.axis_index("grp") // (group_count // 2) % 2
    mine_first = upper_half * half_heads
    other_first = (1 - upper_half) * half_heads
    key_heads = key_rows.reshape(row_count, KVH, DH)
    value_heads = value_rows.reshape(row_count, KVH, DH)

    def select(array, first):
        return lax.dynamic_slice_in_dim(array, first, half_heads, 1)

    query_width = half_heads * ratio * DH
    key_width = half_heads * DH
    outgoing = jnp.concatenate(
        [
            select(query, other_first).reshape(row_count, query_width),
            select(key_heads, other_first).reshape(row_count, key_width),
            select(value_heads, other_first).reshape(row_count, key_width),
        ],
        1,
    )
    incoming, partner_doc = partner((outgoing, doc_row), "grp", pair_bit)
    partner_query = incoming[:, :query_width].reshape(row_count, half_heads, ratio, DH)
    partner_keys = incoming[:, query_width : query_width + key_width]
    partner_values = incoming[:, query_width + key_width :]
    own_query = select(query, mine_first)
    own_keys = select(key_heads, mine_first).reshape(row_count, key_width)
    own_values = select(value_heads, mine_first).reshape(row_count, key_width)
    own_update = make_update(own_query, positions, doc_row)
    partner_update = make_update(partner_query, positions, partner_doc)
    carries = (initial(own_query), initial(partner_query))
    offset = jnp.int32(0)
    carries = (
        own_update(
            carries[0],
            lax.all_gather(own_keys, "ctx", axis=0, tiled=True),
            lax.all_gather(own_values, "ctx", axis=0, tiled=True),
            lax.all_gather(doc_row, "ctx", axis=0, tiled=True),
            offset,
        ),
        partner_update(
            carries[1],
            lax.all_gather(partner_keys, "ctx", axis=0, tiled=True),
            lax.all_gather(partner_values, "ctx", axis=0, tiled=True),
            lax.all_gather(partner_doc, "ctx", axis=0, tiled=True),
            offset,
        ),
    )
    own_out, own_log = finish(carries[0])
    partner_out, partner_log = finish(carries[1])
    back_out, back_log = (
        partner(partner_out, "grp", pair_bit),
        partner(partner_log.astype(jnp.bfloat16), "grp", pair_bit).astype(partner_log.dtype),
    )
    is_lower = upper_half == 0
    lower_out = jnp.where(is_lower, own_out, back_out)
    higher_out = jnp.where(is_lower, back_out, own_out)
    lower_log = jnp.where(is_lower, own_log, back_log)
    higher_log = jnp.where(is_lower, back_log, own_log)
    attended = jnp.concatenate([lower_out, higher_out], 1)
    log_totals = jnp.concatenate([lower_log, higher_log], 0)
    return (attended.reshape(row_count, QH * DH), log_totals)


def solution(mesh):
    placed = (
        P(("grp", "ctx"), None),
        P(("grp", "ctx"), None),
        P(("grp", "ctx"), None),
        P("grp", "ctx"),
    )
    return jax.shard_map(
        per_device,
        mesh=mesh,
        in_specs=placed,
        out_specs=(P(("grp", "ctx"), None), P(None, ("grp", "ctx"))),
        check_vma=False,
    )
```

profile of v0, /device:TPU:32, one launch (start us, length us, event | category | flops | bytes accessed | tf_op | source)
XLA Modules:
  0.0 670.8 jit_solution(9183439023123077032)
XLA Ops:
  7.2 0.9 reshape.79
  8.1 0.9 reshape.77
  10.6 1.1 copy.48
  11.9 4.9 collective-permute-start.1
  16.9 7.9 %collective-permute-done.1 = bf16[64,2560]{1,0:T(8,128)(2,1)S(1)} collective-permute-done((bf16[64,2560]{1,0:T(8,128)(2,1)S(1)}, bf16[64,2560]{1,0:T(8,128)(2,1)S(1)}, u32[]{:S(2)}, u32[]{:S(2)}) %collective-permute-start.1) | collective-permute-done | bytes 327712 | tf_op jit(solution)/shard_map/ppermute | solution.py:18
  26.0 4.9 collective-permute-start
  31.0 1.3 dynamic-slice
  35.2 153.3 %all-reduce.2 = (s32[2048]{0:T(1024)S(1)}, s32[2048]{0:T(1024)S(1)}) all-reduce(s32[2048]{0:T(1024)S(1)} %dynamic-update-slice.1, s32[2048]{0:T(1024)S(1)} %bitcast_dynamic-update-slice_fusion), channel_id=1, replica_groups=mesh['grp'=16,'ctx'=32] {'ctx'}, use_global_device_ids=true, to_apply=%add.1 | all-reduce | flops 4096 | bytes 32768
  191.7 129.7 %all-gather.8.cloned.1.call-done = bf16[2048,256]{1,0:T(8,128)(2,1)} async-done(((bf16[64,256]{1,0:T(8,128)(2,1)}), bf16[2048,256]{1,0:T(8,128)(2,1)}) %all-gather.8.cloned.1.call-update) | async-done | bytes 1048592 | tf_op jit(solution)/shard_map/all_gather | solution.py:124
  321.4 17.7 %conditional.2 = (f32[2,8,64]{1,2,0:T(8,128)}, f32[2,8,64]{1,2,0:T(8,128)}, f32[2,8,64]{1,2,0:T(8,128)S(1)}, f32[2,8,64,128]{3,2,1,0:T(8,128)S(1)}) conditional(s32[]{:T(128)} %convert_element_type.28, () %tuple.30, (s32[64]{0:T(128)S(1)}, s32[2048]{0:T(1024)S(1)}, s32[1,64]{1,0:T(1,128)}, bf16[64,4,8,128]{3,2,1,0:T(8,128)(2,1)S(1)}, s32[]{:T(128)}, ...), branch_computations={%region_1.2_spmd, %region_2.5_spmd} | conditional | flops 1097202688 | bytes 71606880 | solution.py:59
  321.4 0.8 fusion.11
  322.2 1.3 reshape.61
  323.6 2.2 fusion
  326.4 2.6 copy-done.1
  329.0 4.3 fusion.4
  333.3 0.9 log.11
  334.5 4.5 fusion.5
  339.1 0.9 copy.29
  340.0 0.9 add.32
  340.9 135.3 %all-gather.10.cloned.1.call-done = bf16[2048,256]{1,0:T(8,128)(2,1)} async-done(((bf16[64,256]{1,0:T(8,128)(2,1)}), bf16[2048,256]{1,0:T(8,128)(2,1)}) %all-gather.10.cloned.1.call-update) | async-done | bytes 1048592 | tf_op jit(solution)/shard_map/all_gather | solution.py:130
  476.3 154.7 %all-gather.12.cloned.1.call-done = bf16[2048,256]{1,0:T(8,128)(2,1)} async-done(((bf16[64,256]{1,0:T(8,128)(2,1)}), bf16[2048,256]{1,0:T(8,128)(2,1)}) %all-gather.12.cloned.1.call-update) | async-done | bytes 1048592 | tf_op jit(solution)/shard_map/all_gather | solution.py:131
  630.9 15.5 %conditional.3 = (f32[2,8,64]{2,1,0:T(8,128)}, f32[2,8,64]{2,1,0:T(8,128)}, f32[2,8,64,128]{3,2,1,0:T(8,128)S(1)}, f32[2,8,64]{2,1,0:T(8,128)S(1)}) conditional(s32[]{:T(128)} %convert_element_type.30, () %tuple.32, (s32[64]{0:T(128)S(1)}, s32[2048]{0:T(1024)S(1)}, s32[64]{0:T(128)S(1)}, bf16[2048,256]{1,0:T(8,128)(2,1)}, ...), branch_computations={%region_6.7_spmd, %region_7.10_spmd} | conditional | flops 1097202688 | bytes 71606872 | solution.py:59
  631.2 1.3 reshape.63
  632.6 1.7 fusion.16
  634.9 2.6 copy-done
  637.5 3.5 fusion.20
  641.3 4.4 fusion.21
  647.2 4.8 collective-permute-start.3
  652.0 0.9 fusion.31
  652.9 2.5 collective-permute-start.2
  656.1 6.6 collective-permute-done.2
  663.3 1.0 copy.80
  (50 shorter events, 10.8 us)
Async XLA Ops:
  7.2 184.5 %all-gather.6.cloned.1.call-start = ((), (), s32[]{:S(2)}) async-start(), calls=%async_computation | async-start | bytes 1081344 | tf_op jit(solution)/shard_map/all_gather | solution.py:123
  9.8 311.6 %all-gather.8.cloned.1.call-start = ((), (), s32[]{:S(2)}) async-start(), calls=%async_computation.1 | async-start | bytes 1081344 | tf_op jit(solution)/shard_map/all_gather | solution.py:124
  10.5 465.7 %all-gather.10.cloned.1.call-start = ((), (), s32[]{:S(2)}) async-start(), calls=%async_computation.2 | async-start | bytes 1081344 | tf_op jit(solution)/shard_map/all_gather | solution.py:130
  11.9 12.8 %collective-permute-start.1 = (bf16[64,2560]{1,0:T(8,128)(2,1)S(1)}, bf16[64,2560]{1,0:T(8,128)(2,1)S(1)}, u32[]{:S(2)}, u32[]{:S(2)}) collective-permute-start(bf16[64,2560]{1,0:T(8,128)(2,1)S(1)} %pad_maximum_fusion.1), channel_id=1, source_target_pairs={{0,256},{256,0},{32,288},{288,32},{64,320},{320,64},{96,352},{352,... | collective-permute-start | bytes 983048 | tf_op jit(solution)/shard_map/ppermute | solution.py:18
  25.4 605.5 %all-gather.12.cloned.1.call-start = ((), (), s32[]{:S(2)}) async-start(), calls=%async_computation.3 | async-start | bytes 1081344 | tf_op jit(solution)/shard_map/all_gather | solution.py:131
  26.0 8.9 %collective-permute-start = (s32[64]{0:T(128)}, s32[64]{0:T(128)S(1)}, u32[]{:S(2)}, u32[]{:S(2)}) collective-permute-start(s32[64]{0:T(128)} %bitcast.104), channel_id=1, source_target_pairs={{0,256},{256,0},{32,288},{288,32},{64,320},{320,64},{96,352},{352,... | collective-permute-start | bytes 776 | tf_op jit(solution)/shard_map/ppermute | solution.py:18
  323.6 10.6 %copy-start.3 = (bf16[2048,256]{1,0:T(8,128)(2,1)S(1)}, bf16[2048,256]{1,0:T(8,128)(2,1)}, u32[]{:S(2)}) copy-start(bf16[2048,256]{1,0:T(8,128)(2,1)} %get-tuple-element.56) | copy-start | bytes 3145732 | tf_op jit(solution)/shard_map/cond
  325.8 3.2 copy-start.1
  632.6 8.5 %copy-start.2 = (bf16[2048,256]{1,0:T(8,128)(2,1)S(1)}, bf16[2048,256]{1,0:T(8,128)(2,1)}, u32[]{:S(2)}) copy-start(bf16[2048,256]{1,0:T(8,128)(2,1)} %get-tuple-element.62) | copy-start | bytes 3145732 | tf_op jit(solution)/shard_map/cond
  634.3 3.2 copy-start
  647.2 8.3 %collective-permute-start.3 = (bf16[16,64]{1,0:T(8,128)(2,1)S(1)}, bf16[16,64]{1,0:T(8,128)(2,1)S(1)}, u32[]{:S(2)}, u32[]{:S(2)}) collective-permute-start(bf16[16,64]{1,0:T(8,128)(2,1)S(1)} %fusion.32), channel_id=1, source_target_pairs={{0,256},{256,0},{32,288},{288,32},{64,320},{320,64},{96,352},{352,... | collective-permute-start | bytes 6152 | tf_op jit(solution)/shard_map/ppermute | solution.py:18
  652.9 9.8 %collective-permute-start.2 = (bf16[64,2,8,128]{3,0,2,1:T(8,128)(2,1)S(1)}, bf16[64,2,8,128]{3,0,2,1:T(8,128)(2,1)S(1)}, u32[]{:S(2)}, u32[]{:S(2)}) collective-permute-start(bf16[64,2,8,128]{3,0,2,1:T(8,128)(2,1)S(1)} %fusion.31), channel_id=1, source_target_pairs={{0,256},{256,0},{32,288},{288,32},{64,320},{320,64},{96,352},{352,... | collective-permute-start | bytes 786440 | tf_op jit(solution)/shard_map/ppermute | solution.py:18
Sparse Core Ops, SparseCore 0:
  10.7 155.8 all-gather.5
  168.6 152.7 all-gather.7
  323.5 152.7 all-gather.9
  478.2 152.7 all-gather.11
where the time goes:
time: 672 us; the launch traced here: 671 us
  waiting for transfers between devices  435 us (65%)
  blocking collectives  153 us (23%)
  local copies, waits for them, and re-layouts  20.3 us (3%)
  starting transfers between devices  17.4 us (3%)
  between operations  17.3 us (3%)
  other arithmetic  14.8 us (2%)
  matrix products  12.8 us (2%)
    all_gather x1, waiting for transfers between devices, per_device(): lax.all_gather(partner_values, 'ctx', axis=0, tiled=True)  155 us
    unnamed x1, blocking collectives  153 us
    all_gather x1, waiting for transfers between devices, per_device(): lax.all_gather(partner_keys, 'ctx', axis=0, tiled=True)  135 us
    all_gather x1, waiting for transfers between devices, per_device(): lax.all_gather(own_values, 'ctx', axis=0, tiled=True)  130 us
    ppermute x4, starting transfers between devices, partner(): return lax.ppermute(block, axis, route)  17.2 us
    ppermute x4, waiting for transfers between devices, partner(): return lax.ppermute(block, axis, route)  14.5 us
  transfers between devices with their start and end apart: 8, of which 5 were waited for; matrix products, arithmetic and copies ran while one was open for 4% of the time, Pallas kernels for 0%

commit v1 on v0

v1 whole, which is shorter than its diff:
```python
import functools
import math

import jax
import jax.numpy as jnp
from jax import lax
from jax.experimental import pallas as pl
from jax.experimental.pallas import tpu as pltpu
from jax.sharding import Mesh, PartitionSpec as P

QH = 32
KVH = 4
DH = 128
RATIO = QH // KVH
ROWS = 8
COLS = 4
MOST = 1024
NEG = -1e30


def attend_kernel(row_ref, q_ref, own_ref, *rest):
    halo_refs = rest[:-3]
    out_ref, bias_ref, value_ref = rest[-3:]
    tokens = q_ref.shape[0]
    chunks = (own_ref,) + tuple(halo_refs)
    row = row_ref[0]
    own_docs = own_ref[tokens:, :].astype(jnp.float32)
    doc_col = own_docs.T[:, :1]
    q_pos = lax.broadcasted_iota(jnp.int32, (tokens, tokens), 0)
    k_pos = lax.broadcasted_iota(jnp.int32, (tokens, tokens), 1)
    for i, chunk in enumerate(chunks):
        doc_row = chunk[tokens:, :].astype(jnp.float32)[:1]
        allowed = doc_col == doc_row
        if i == 0:
            allowed = allowed & (k_pos <= q_pos)
        else:
            allowed = allowed & (row >= i)
        bias_ref[i] = jnp.where(allowed, 0.0, NEG)
        value_ref[i, :, :DH] = chunk[:tokens, DH:]
        value_ref[i, :, DH:] = jnp.ones((tokens, DH), jnp.bfloat16)
    scale = 1.0 / math.sqrt(DH)
    scale2 = scale * math.log2(math.e)
    lanes = lax.broadcasted_iota(jnp.int32, (tokens, DH), 1)
    logs = jnp.zeros((tokens, DH), jnp.float32)
    for head in range(RATIO):
        query = q_ref[:, head * DH : (head + 1) * DH]
        scores = []
        for i, chunk in enumerate(chunks):
            product = lax.dot_general(
                query,
                chunk[:tokens, :DH],
                (((1,), (1,)), ((), ())),
                preferred_element_type=jnp.float32,
            )
            scores.append(product + bias_ref[i])
        top = functools.reduce(jnp.maximum, scores)
        row_max = jnp.max(top, axis=1, keepdims=True)
        total = jnp.zeros((tokens, 2 * DH), jnp.float32)
        for i in range(len(chunks)):
            weights = jnp.exp2((scores[i] - row_max) * scale2).astype(jnp.bfloat16)
            total += jnp.dot(weights, value_ref[i], preferred_element_type=jnp.float32)
        denominator = total[:, DH:]
        out_ref[:, head * DH : (head + 1) * DH] = (total[:, :DH] / denominator).astype(jnp.bfloat16)
        log_total = row_max * scale + jnp.log(denominator)
        high = log_total.astype(jnp.bfloat16).astype(jnp.float32)
        logs = jnp.where(lanes == head, high, logs)
        logs = jnp.where(lanes == RATIO + head, log_total - high, logs)
    out_ref[:, RATIO * DH :] = logs.astype(jnp.bfloat16)


def attend(row, query, own, halo):
    tokens = query.shape[0]
    count = 1 + len(halo)
    whole = pl.BlockSpec(memory_space=pltpu.VMEM)
    return pl.pallas_call(
        attend_kernel,
        out_shape=jax.ShapeDtypeStruct((tokens, (RATIO + 1) * DH), jnp.bfloat16),
        in_specs=[pl.BlockSpec(memory_space=pltpu.SMEM)] + [whole] * (1 + count),
        out_specs=whole,
        scratch_shapes=[
            pltpu.VMEM((count, tokens, tokens), jnp.float32),
            pltpu.VMEM((count, tokens, 2 * DH), jnp.bfloat16),
        ],
        compiler_params=pltpu.CompilerParams(vmem_limit_bytes=48 * 1024 * 1024),
        cost_estimate=pl.CostEstimate(
            flops=4 * RATIO * tokens * tokens * count * DH * 2,
            bytes_accessed=3 * 1024 * 1024,
            transcendentals=RATIO * tokens * tokens * count,
        ),
    )(row, query, own, *halo)


def per_device(queries, key_rows, value_rows, doc_ids):
    count = queries.shape[0]
    tokens = count * COLS
    row = lax.axis_index("y")
    keys = key_rows.reshape(count, KVH, DH)
    values = value_rows.reshape(count, KVH, DH)
    pairs = jnp.transpose(jnp.concatenate([keys, values], 2), (1, 0, 2))
    docs = jnp.pad(doc_ids.astype(jnp.bfloat16), ((0, 15), (0, 2 * DH - count)))
    docs = jnp.broadcast_to(docs[None], (KVH, 16, 2 * DH))
    sent = jnp.concatenate([pairs, docs], 1)
    got = lax.all_to_all(sent, "z", 0, 0, tiled=True)
    doc_line = got[:, count, :count].reshape(1, tokens)
    own = jnp.concatenate(
        [got[:, :count].reshape(tokens, 2 * DH), jnp.broadcast_to(doc_line, (16, tokens))], 0
    )
    halo = []
    for back in range(1, MOST // tokens + 1):
        route = [(low, low + back) for low in range(ROWS - back)]
        halo.append(lax.ppermute(own, "y", route))
    query = jnp.transpose(queries.reshape(count, KVH, RATIO * DH), (1, 0, 2))
    query = lax.all_to_all(query, "z", 0, 0, tiled=True).reshape(tokens, RATIO * DH)
    out = attend(row.reshape(1), query, own, halo)
    back = lax.all_to_all(out.reshape(COLS, count, (RATIO + 1) * DH), "z", 0, 0, tiled=True)
    attended = jnp.transpose(back[:, :, : RATIO * DH], (1, 0, 2)).reshape(count, QH * DH)
    logs = back[:, :, RATIO * DH : RATIO * DH + 2 * RATIO].astype(jnp.float32)
    logs = logs[:, :, :RATIO] + logs[:, :, RATIO:]
    return attended, jnp.transpose(logs, (0, 2, 1)).reshape(QH, count)


def solution(mesh):
    names = ("grp", "y", "z")
    split = Mesh(mesh.devices.reshape(mesh.shape["grp"], ROWS, COLS), names)
    block = P(names, None)
    return jax.shard_map(
        per_device,
        mesh=split,
        in_specs=(block, block, block, P("grp", ("y", "z"))),
        out_specs=(block, P(None, names)),
        check_vma=False,
    )
```

time: 672 us -> 76.6 us (0.11)
  the two profiles are of different devices: /device:TPU:32 before, /device:TPU:36 now
where the time goes in v1:
time: 76.6 us; the launch traced here: 76.2 us
  waiting for transfers between devices  26.8 us (35%)
  blocking collectives  20.7 us (27%)
  starting transfers between devices  18.7 us (24%)
  local copies, waits for them, and re-layouts  4.15 us (5%)
  Pallas kernels  4.1 us (5%)
  other arithmetic  0.96 us (1%)
  between operations  0.78 us (1%)
    ppermute x4, waiting for transfers between devices, per_device(): halo.append(lax.ppermute(own, 'y', route))  21.3 us
    all_to_all x1, blocking collectives, per_device(): lax.all_to_all(out.reshape(COLS, count, (RATIO + 1) * DH), 'z', 0, 0, til...  20.7 us
    ppermute x4, starting transfers between devices, per_device(): halo.append(lax.ppermute(own, 'y', route))  7.95 us
    all_to_all x1, starting transfers between devices, per_device(): got = lax.all_to_all(sent, 'z', 0, 0, tiled=True)  7.26 us
    all_to_all x1, waiting for transfers between devices, per_device(): got = lax.all_to_all(sent, 'z', 0, 0, tiled=True)  5.59 us
    pallas_call x1, Pallas kernels, attend(): pl.pallas_call(attend_kernel, out_shape=jax.ShapeDtypeStruct((tokens, (RA...  4.1 us
    all_to_all x1, starting transfers between devices, per_device(): lax.all_to_all(query, 'z', 0, 0, tiled=True).reshape(tokens, RATIO * DH)  3.47 us
  transfers between devices with their start and end apart: 6, of which 5 were waited for; matrix products, arithmetic and copies ran while one was open for 1% of the time, Pallas kernels for 0%

profile of v1, /device:TPU:36, one launch (start us, length us, event | category | flops | bytes accessed | tf_op | source)
XLA Modules:
  0.0 76.2 jit_solution(4459400805203433827)
XLA Ops:
  0.6 0.7 convert_element_type.8
  1.3 0.0 copy-start.1
  1.3 0.9 %reshape.36 = bf16[64,4,128]{2,1,0:T(4,128)(2,1)S(1)} reshape(bf16[64,512]{1,0:T(8,128)(2,1)} %param.5) | data formatting | bytes 131072 | tf_op jit(solution)/shard_map/reshape | solution.py:97
  2.2 0.0 copy-done.1
  2.2 0.1 maximum_bitcast_fusion
  2.3 0.0 copy-start
  2.3 0.1 pad_maximum_fusion
  2.5 0.7 copy.19
  3.1 7.3 %all-to-all-start.1 = ((bf16[4,80,256]{2,1,0:T(8,128)(2,1)}), bf16[4,80,256]{2,1,0:T(8,128)(2,1)S(1)}, u32[]{:S(2)}, u32[]{:S(2)}) async-start(bf16[4,80,256]{2,1,0:T(8,128)(2,1)} %copy.19), calls=%async_computation.1 | async-start | bytes 327680 | tf_op jit(solution)/shard_map/all_to_all | solution.py:103
  10.4 0.0 copy-done
  10.4 0.8 %copy.25 = bf16[8,4,8,1024]{3,2,0,1:T(8,128)(2,1)} copy(bf16[8,4,8,1024]{3,2,1,0:T(8,128)(2,1)S(1)} %bitcast.22) | data formatting | bytes 1048576 | tf_op jit(solution)/shard_map/reshape | solution.py:112
  11.2 5.6 %all-to-all-done.1 = bf16[4,80,256]{2,1,0:T(8,128)(2,1)S(1)} async-done(((bf16[4,80,256]{2,1,0:T(8,128)(2,1)}), bf16[4,80,256]{2,1,0:T(8,128)(2,1)S(1)}, u32[]{:S(2)}, u32[]{:S(2)}) %all-to-all-start.1) | async-done | bytes 163872 | tf_op jit(solution)/shard_map/all_to_all | solution.py:103
  16.8 3.5 %all-to-all-start = ((bf16[4,64,1024]{2,1,0:T(8,128)(2,1)}), bf16[4,64,1024]{2,1,0:T(8,128)(2,1)S(1)}, u32[]{:S(2)}, u32[]{:S(2)}) async-start(bf16[4,64,1024]{2,1,0:T(8,128)(2,1)} %bitcast.19), calls=%async_computation | async-start | bytes 1048576 | tf_op jit(solution)/shard_map/all_to_all | solution.py:113
  20.3 0.1 broadcast_in_dim.14
  20.4 1.3 %collective-permute-start.3 = (bf16[272,256]{1,0:T(8,128)(2,1)S(1)}, bf16[272,256]{1,0:T(8,128)(2,1)S(1)}, u32[]{:S(2)}, u32[]{:S(2)}) collective-permute-start(bf16[272,256]{1,0:T(8,128)(2,1)S(1)} %pad_maximum_fusion.1.own_ref), channel_id=1, source_target_pairs={{0,16},{4,20},{8,24},{12,28},{1,17},{5,21},{9,25},{13,29},{2,18},{... | collective-permute-start | bytes 417800 | tf_op jit(solution)/shard_map/ppermute | solution.py:111
  21.7 2.8 %collective-permute-start.2 = (bf16[272,256]{1,0:T(8,128)(2,1)S(1)}, bf16[272,256]{1,0:T(8,128)(2,1)S(1)}, u32[]{:S(2)}, u32[]{:S(2)}) collective-permute-start(bf16[272,256]{1,0:T(8,128)(2,1)S(1)} %pad_maximum_fusion.1.own_ref), channel_id=1, source_target_pairs={{0,12},{4,16},{8,20},{12,24},{16,28},{1,13},{5,17},{9,21},{13,25},... | collective-permute-start | bytes 417800 | tf_op jit(solution)/shard_map/ppermute | solution.py:111
  24.6 1.9 %collective-permute-start.1 = (bf16[272,256]{1,0:T(8,128)(2,1)S(1)}, bf16[272,256]{1,0:T(8,128)(2,1)S(1)}, u32[]{:S(2)}, u32[]{:S(2)}) collective-permute-start(bf16[272,256]{1,0:T(8,128)(2,1)S(1)} %pad_maximum_fusion.1.own_ref), channel_id=1, source_target_pairs={{0,8},{4,12},{8,16},{12,20},{16,24},{20,28},{1,9},{5,13},{9,17},{1... | collective-permute-start | bytes 417800 | tf_op jit(solution)/shard_map/ppermute | solution.py:111
  26.5 1.9 %collective-permute-start = (bf16[272,256]{1,0:T(8,128)(2,1)S(1)}, bf16[272,256]{1,0:T(8,128)(2,1)S(1)}, u32[]{:S(2)}, u32[]{:S(2)}) collective-permute-start(bf16[272,256]{1,0:T(8,128)(2,1)S(1)} %pad_maximum_fusion.1.own_ref), channel_id=1, source_target_pairs={{0,4},{4,8},{8,12},{12,16},{16,20},{20,24},{24,28},{1,5},{5,9},{9,... | collective-permute-start | bytes 417800 | tf_op jit(solution)/shard_map/ppermute | solution.py:111
  28.4 4.4 %collective-permute-done.3.rest_3_ = bf16[272,256]{1,0:T(8,128)(2,1)S(1)} collective-permute-done((bf16[272,256]{1,0:T(8,128)(2,1)S(1)}, bf16[272,256]{1,0:T(8,128)(2,1)S(1)}, u32[]{:S(2)}, u32[]{:S(2)}) %collective-permute-start.3) | collective-permute-done | bytes 139296 | tf_op jit(solution)/shard_map/ppermute | solution.py:111
  32.8 7.6 %collective-permute-done.2.rest_2_ = bf16[272,256]{1,0:T(8,128)(2,1)S(1)} collective-permute-done((bf16[272,256]{1,0:T(8,128)(2,1)S(1)}, bf16[272,256]{1,0:T(8,128)(2,1)S(1)}, u32[]{:S(2)}, u32[]{:S(2)}) %collective-permute-start.2) | collective-permute-done | bytes 139296 | tf_op jit(solution)/shard_map/ppermute | solution.py:111
  40.4 7.8 %collective-permute-done.1.rest_1_ = bf16[272,256]{1,0:T(8,128)(2,1)S(1)} collective-permute-done((bf16[272,256]{1,0:T(8,128)(2,1)S(1)}, bf16[272,256]{1,0:T(8,128)(2,1)S(1)}, u32[]{:S(2)}, u32[]{:S(2)}) %collective-permute-start.1) | collective-permute-done | bytes 139296 | tf_op jit(solution)/shard_map/ppermute | solution.py:111
  48.3 1.4 %collective-permute-done.rest_0_ = bf16[272,256]{1,0:T(8,128)(2,1)S(1)} collective-permute-done((bf16[272,256]{1,0:T(8,128)(2,1)S(1)}, bf16[272,256]{1,0:T(8,128)(2,1)S(1)}, u32[]{:S(2)}, u32[]{:S(2)}) %collective-permute-start) | collective-permute-done | bytes 139296 | tf_op jit(solution)/shard_map/ppermute | solution.py:111
  49.7 0.0 all-to-all-done
  49.7 4.1 %shard_map.59 = bf16[256,1152]{1,0:T(8,128)(2,1)S(1)} custom-call(s32[1]{0:T(128)} %bitcast.row_ref, bf16[256,1024]{1,0:T(8,128)(2,1)S(1)} %bitcast.21, bf16[272,256]{1,0:T(8,128)(2,1)S(1)} %pad_maximum_fusion.1.own_ref, bf16[272,256]{1,0:T(8,128)(2,1)S(1)} %collective-permute-done.rest_0_, bf16[272,256]{1,0:T(8,128)(2,1)S(1)} %collective-permute-done.1.rest_1_, ...), custom_call_target="tpu_custom_call" | custom-call | flops 2684354560 | bytes 3145728 | tf_op jit(solution)/shard_map/pallas_call | solution.py:75
  53.8 20.7 %all_to_all.15 = bf16[4,64,1152]{2,1,0:T(8,128)(2,1)S(1)} all-to-all(bf16[4,64,1152]{2,1,0:T(8,128)(2,1)S(1)} %bitcast.20), channel_id=1, replica_groups=mesh['grp'=16,'y'=8,'z'=4] {'z'}, dimensions={0} | all-to-all | bytes 1179648 | tf_op jit(solution)/shard_map/all_to_all | solution.py:115
  74.5 0.1 slice_bitcast_fusion
  74.5 0.8 %copy.23 = bf16[4,8,8,1024]{3,2,0,1:T(8,128)(2,1)} copy(bf16[4,8,8,1024]{3,2,1,0:T(8,128)(2,1)S(1)} %slice_bitcast_fusion) | data formatting | bytes 1048576 | tf_op jit(solution)/shard_map/reshape | solution.py:116
  75.4 0.1 fusion
  75.5 0.7 copy.21
  (8 shorter events, 0.1 us)
Async XLA Ops:
  1.3 0.9 %copy-start.1 = (bf16[64,512]{1,0:T(8,128)(2,1)S(1)}, bf16[64,512]{1,0:T(8,128)(2,1)}, u32[]{:S(2)}) copy-start(bf16[64,512]{1,0:T(8,128)(2,1)} %param.6) | copy-start | bytes 196612
  2.3 8.1 %copy-start = (bf16[64,4096]{1,0:T(8,128)(2,1)S(1)}, bf16[64,4096]{1,0:T(8,128)(2,1)}, u32[]{:S(2)}) copy-start(bf16[64,4096]{1,0:T(8,128)(2,1)} %param.4) | copy-start | bytes 1572868
  3.1 13.7 %all-to-all-start.1 = ((bf16[4,80,256]{2,1,0:T(8,128)(2,1)}), bf16[4,80,256]{2,1,0:T(8,128)(2,1)S(1)}, u32[]{:S(2)}, u32[]{:S(2)}) async-start(bf16[4,80,256]{2,1,0:T(8,128)(2,1)} %copy.19), calls=%async_computation.1 | async-start | bytes 327680 | tf_op jit(solution)/shard_map/all_to_all | solution.py:103
  16.8 32.9 %all-to-all-start = ((bf16[4,64,1024]{2,1,0:T(8,128)(2,1)}), bf16[4,64,1024]{2,1,0:T(8,128)(2,1)S(1)}, u32[]{:S(2)}, u32[]{:S(2)}) async-start(bf16[4,64,1024]{2,1,0:T(8,128)(2,1)} %bitcast.19), calls=%async_computation | async-start | bytes 1048576 | tf_op jit(solution)/shard_map/all_to_all | solution.py:113
  20.4 12.4 %collective-permute-start.3 = (bf16[272,256]{1,0:T(8,128)(2,1)S(1)}, bf16[272,256]{1,0:T(8,128)(2,1)S(1)}, u32[]{:S(2)}, u32[]{:S(2)}) collective-permute-start(bf16[272,256]{1,0:T(8,128)(2,1)S(1)} %pad_maximum_fusion.1.own_ref), channel_id=1, source_target_pairs={{0,16},{4,20},{8,24},{12,28},{1,17},{5,21},{9,25},{13,29},{2,18},{... | collective-permute-start | bytes 417800 | tf_op jit(solution)/shard_map/ppermute | solution.py:111
  21.7 18.7 %collective-permute-start.2 = (bf16[272,256]{1,0:T(8,128)(2,1)S(1)}, bf16[272,256]{1,0:T(8,128)(2,1)S(1)}, u32[]{:S(2)}, u32[]{:S(2)}) collective-permute-start(bf16[272,256]{1,0:T(8,128)(2,1)S(1)} %pad_maximum_fusion.1.own_ref), channel_id=1, source_target_pairs={{0,12},{4,16},{8,20},{12,24},{16,28},{1,13},{5,17},{9,21},{13,25},... | collective-permute-start | bytes 417800 | tf_op jit(solution)/shard_map/ppermute | solution.py:111
  24.6 23.7 %collective-permute-start.1 = (bf16[272,256]{1,0:T(8,128)(2,1)S(1)}, bf16[272,256]{1,0:T(8,128)(2,1)S(1)}, u32[]{:S(2)}, u32[]{:S(2)}) collective-permute-start(bf16[272,256]{1,0:T(8,128)(2,1)S(1)} %pad_maximum_fusion.1.own_ref), channel_id=1, source_target_pairs={{0,8},{4,12},{8,16},{12,20},{16,24},{20,28},{1,9},{5,13},{9,17},{1... | collective-permute-start | bytes 417800 | tf_op jit(solution)/shard_map/ppermute | solution.py:111
  26.5 23.2 %collective-permute-start = (bf16[272,256]{1,0:T(8,128)(2,1)S(1)}, bf16[272,256]{1,0:T(8,128)(2,1)S(1)}, u32[]{:S(2)}, u32[]{:S(2)}) collective-permute-start(bf16[272,256]{1,0:T(8,128)(2,1)S(1)} %pad_maximum_fusion.1.own_ref), channel_id=1, source_target_pairs={{0,4},{4,8},{8,12},{12,16},{16,20},{20,24},{24,28},{1,5},{5,9},{9,... | collective-permute-start | bytes 417800 | tf_op jit(solution)/shard_map/ppermute | solution.py:111

commit v2 on v1

v2 whole, which is shorter than its diff:
```python
import functools
import math

import jax
import jax.numpy as jnp
from jax import lax
from jax.experimental import pallas as pl
from jax.experimental.pallas import tpu as pltpu
from jax.sharding import Mesh, PartitionSpec as P

QH = 32
KVH = 4
DH = 128
RATIO = QH // KVH
ROWS = 8
COLS = 4
NEG = -1e30
VMEM = pl.BlockSpec(memory_space=pltpu.VMEM)
SMEM = pl.BlockSpec(memory_space=pltpu.SMEM)
ANY = pl.BlockSpec(memory_space=pl.ANY)


def params():
    return pltpu.CompilerParams(vmem_limit_bytes=40 * 1024 * 1024)


def pack_kernel(k_ref, v_ref, doc_ref, out_ref, line_ref, sems):
    count = k_ref.shape[0]
    copies = [pltpu.make_async_copy(doc_ref, line_ref, sems.at[0])]
    for head in range(COLS):
        part = slice(head * DH, (head + 1) * DH)
        for side, ref in enumerate((k_ref, v_ref)):
            target = out_ref.at[head, :count, side * DH : (side + 1) * DH]
            copies.append(pltpu.make_async_copy(ref.at[:, part], target, sems.at[1 + 2 * head + side]))
    for copy in copies:
        copy.start()
    copies[0].wait()
    docs = jnp.broadcast_to(line_ref[...].astype(jnp.float32), (16, count)).astype(jnp.bfloat16)
    for head in range(COLS):
        out_ref[head, count:, :] = jnp.zeros((16, 2 * DH), jnp.bfloat16)
        out_ref[head, count:, :count] = docs
    for copy in copies[1:]:
        copy.wait()


def pack(key_rows, value_rows, doc_ids):
    count = key_rows.shape[0]
    return pl.pallas_call(
        pack_kernel,
        out_shape=jax.ShapeDtypeStruct((COLS, count + 16, 2 * DH), jnp.bfloat16),
        in_specs=[ANY, ANY, ANY],
        out_specs=VMEM,
        scratch_shapes=[
            pltpu.VMEM(doc_ids.shape, doc_ids.dtype),
            pltpu.SemaphoreType.DMA((1 + 2 * COLS,)),
        ],
        compiler_params=pltpu.CompilerParams(vmem_limit_bytes=63 * 1024 * 1024),
    )(key_rows, value_rows, doc_ids)


def attend_kernel(row_ref, q_ref, *refs):
    out_ref, bias_ref, value_ref = refs[-3:]
    chunks = refs[:-3]
    count = q_ref.shape[1]
    tokens = count * COLS
    row = row_ref[0]
    doc_col = chunks[0][tokens:, :].astype(jnp.float32).T[:, :1]
    q_pos = lax.broadcasted_iota(jnp.int32, (tokens, tokens), 0)
    k_pos = lax.broadcasted_iota(jnp.int32, (tokens, tokens), 1)
    for i, chunk in enumerate(chunks):
        doc_row = chunk[tokens:, :].astype(jnp.float32)[:1]
        allowed = doc_col == doc_row
        if i == 0:
            allowed = allowed & (k_pos <= q_pos)
        else:
            allowed = allowed & (row >= i)
        bias_ref[i] = jnp.where(allowed, 0.0, NEG)
        value_ref[i, :, :DH] = chunk[:tokens, DH:]
        value_ref[i, :, DH:] = jnp.ones((tokens, DH), jnp.bfloat16)
    scale = 1.0 / math.sqrt(DH)
    scale2 = scale * math.log2(math.e)
    lanes = lax.broadcasted_iota(jnp.int32, (tokens, DH), 1)
    logs = jnp.zeros((tokens, DH), jnp.float32)
    for head in range(RATIO):
        part = slice(head * DH, (head + 1) * DH)
        query = q_ref[:, :, part].reshape(tokens, DH)
        scores = []
        for i, chunk in enumerate(chunks):
            product = lax.dot_general(
                query,
                chunk[:tokens, :DH],
                (((1,), (1,)), ((), ())),
                preferred_element_type=jnp.float32,
            )
            scores.append(product + bias_ref[i])
        top = functools.reduce(jnp.maximum, scores)
        row_max = jnp.max(top, axis=1, keepdims=True)
        total = jnp.zeros((tokens, 2 * DH), jnp.float32)
        for i in range(len(chunks)):
            weights = jnp.exp2((scores[i] - row_max) * scale2).astype(jnp.bfloat16)
            total += jnp.dot(weights, value_ref[i], preferred_element_type=jnp.float32)
        denominator = total[:, DH:]
        mixed = (total[:, :DH] / denominator).astype(jnp.bfloat16)
        out_ref[:, head * count : (head + 1) * count, :] = mixed.reshape(COLS, count, DH)
        log_total = row_max * scale + jnp.log(denominator)
        high = log_total.astype(jnp.bfloat16).astype(jnp.float32)
        logs = jnp.where(lanes == head, high, logs)
        logs = jnp.where(lanes == RATIO + head, log_total - high, logs)
    logs = logs.T[: 2 * RATIO]
    for step in range(COLS):
        piece = logs[:, step * count : (step + 1) * count]
        piece = jnp.concatenate([piece, piece], 1).astype(jnp.bfloat16)
        out_ref[step, RATIO * count :, :] = piece


def attend(row, query, chunks):
    count = query.shape[1]
    tokens = count * COLS
    return pl.pallas_call(
        attend_kernel,
        out_shape=jax.ShapeDtypeStruct((COLS, RATIO * count + 2 * RATIO, DH), jnp.bfloat16),
        in_specs=[SMEM] + [VMEM] * (1 + len(chunks)),
        out_specs=VMEM,
        scratch_shapes=[
            pltpu.VMEM((len(chunks), tokens, tokens), jnp.float32),
            pltpu.VMEM((len(chunks), tokens, 2 * DH), jnp.bfloat16),
        ],
        compiler_params=params(),
    )(row, query, *chunks)


def join_kernel(in_ref, out_ref, log_ref):
    count = out_ref.shape[0]
    for home in range(COLS):
        for head in range(RATIO):
            first = (home * RATIO + head) * DH
            out_ref[:, first : first + DH] = in_ref[home, head * count : (head + 1) * count, :]
        logs = in_ref[home, RATIO * count :, :].astype(jnp.float32)
        logs = logs[:RATIO] + logs[RATIO:]
        log_ref[home * RATIO : (home + 1) * RATIO, :] = logs[:, :count]


def join(blocks, count):
    return pl.pallas_call(
        join_kernel,
        out_shape=[
            jax.ShapeDtypeStruct((count, QH * DH), jnp.bfloat16),
            jax.ShapeDtypeStruct((QH, count), jnp.float32),
        ],
        in_specs=[VMEM],
        out_specs=[VMEM] * 2,
        compiler_params=params(),
    )(blocks)


def per_device(queries, key_rows, value_rows, doc_ids):
    count = queries.shape[0]
    row = lax.axis_index("y").astype(jnp.int32)
    got = lax.all_to_all(pack(key_rows, value_rows, doc_ids), "z", 0, 0, tiled=True)
    own = jnp.concatenate(
        [piece[:count] for piece in got]
        + [jnp.concatenate([piece[count:, :count] for piece in got], 1)],
        0,
    )

    def ahead(array, back, least=0):
        return lax.ppermute(array, "y", [(i, i + back) for i in range(least, ROWS - back)])

    far = lax.ppermute(own, "y", [(i, (i + 6) % ROWS) for i in range(4)])
    chunks = [own] + [ahead(own, back) for back in (1, 2)]
    chunks.append(ahead(chunks[2], 1, 2))
    far = lax.ppermute(far, "y", [((i + 6) % ROWS, i + 4) for i in range(4)])
    chunks.append(far)

    query = jnp.transpose(queries.reshape(count, COLS, RATIO * DH), (1, 0, 2))
    query = lax.all_to_all(query, "z", 0, 0, tiled=True)
    blocks = attend(row.reshape(1), query, chunks)
    blocks = lax.all_to_all(blocks, "z", 0, 0, tiled=True)
    attended, log_totals = join(blocks, count)
    return attended, log_totals


def solution(mesh):
    names = ("grp", "y", "z")
    split_mesh = Mesh(mesh.devices.reshape(mesh.shape["grp"], ROWS, COLS), names)
    block = P(names, None)
    return jax.shard_map(
        per_device,
        mesh=split_mesh,
        in_specs=(block, block, block, P("grp", ("y", "z"))),
        out_specs=(block, P(None, names)),
        check_vma=False,
    )
```

time: 76.6 us -> 61.9 us (0.81)
  the two profiles are of different devices: /device:TPU:36 before, /device:TPU:48 now
where the time goes in v2:
time: 61.9 us; the launch traced here: 61.5 us
  starting transfers between devices  19.8 us (32%)
  waiting for transfers between devices  17.7 us (29%)
  blocking collectives  15.6 us (25%)
  Pallas kernels  6.72 us (11%)
  local copies, waits for them, and re-layouts  0.88 us (1%)
  between operations  0.79 us (1%)
    all_to_all x1, blocking collectives, per_device(): blocks = lax.all_to_all(blocks, 'z', 0, 0, tiled=True)  15.6 us
    all_to_all x1, starting transfers between devices, per_device(): lax.all_to_all(pack(key_rows, value_rows, doc_ids), 'z', 0, 0, tiled=True)  7.27 us
    ppermute x1, waiting for transfers between devices, per_device(): far = lax.ppermute(far, 'y', [((i + 6) % ROWS, i + 4) for i in range(4)])  6.12 us
    ppermute x1, waiting for transfers between devices, per_device(): far = lax.ppermute(own, 'y', [(i, (i + 6) % ROWS) for i in range(4)])  6 us
    ppermute x3, starting transfers between devices, ahead(): lax.ppermute(array, 'y', [(i, i + back) for i in range(least, ROWS - back)])  5.82 us
    all_to_all x1, waiting for transfers between devices, per_device(): lax.all_to_all(pack(key_rows, value_rows, doc_ids), 'z', 0, 0, tiled=True)  5.59 us
    pallas_call x1, Pallas kernels, attend(): pl.pallas_call(attend_kernel, out_shape=jax.ShapeDtypeStruct((COLS, RATIO...  4.2 us
    all_to_all x1, starting transfers between devices, per_device(): query = lax.all_to_all(query, 'z', 0, 0, tiled=True)  3.47 us
  transfers between devices with their start and end apart: 7, of which 3 were waited for; matrix products, arithmetic and copies ran while one was open for 2% of the time, Pallas kernels for 0%

profile of v2, /device:TPU:48, one launch (start us, length us, event | category | flops | bytes accessed | tf_op | source)
XLA Modules:
  0.0 61.5 jit_solution(8196693033292380043)
XLA Ops:
  0.6 0.0 copy-start
  0.6 1.6 %shard_map.59 = bf16[4,80,256]{2,1,0:T(8,128)(2,1)} custom-call(bf16[64,512]{1,0:T(8,128)(2,1)} %k_ref.1, bf16[64,512]{1,0:T(8,128)(2,1)} %v_ref.1, s32[1,64]{1,0:T(1,128)} %doc_ref.1), custom_call_target="tpu_custom_call" | custom-call | tf_op jit(solution)/shard_map/pallas_call | solution.py:48
  2.3 7.3 %all-to-all-start.1 = ((bf16[4,80,256]{2,1,0:T(8,128)(2,1)}), bf16[4,80,256]{2,1,0:T(8,128)(2,1)S(1)}, u32[]{:S(2)}, u32[]{:S(2)}) async-start(bf16[4,80,256]{2,1,0:T(8,128)(2,1)} %shard_map.59), calls=%async_computation.1 | async-start | bytes 327680 | tf_op jit(solution)/shard_map/all_to_all | solution.py:159
  9.5 0.0 copy-done
  9.6 0.8 %copy.9 = bf16[8,4,8,1024]{3,2,0,1:T(8,128)(2,1)} copy(bf16[8,4,8,1024]{3,2,1,0:T(8,128)(2,1)S(1)} %bitcast.32) | data formatting | bytes 1048576 | tf_op jit(solution)/shard_map/reshape | solution.py:175
  10.4 5.6 %all-to-all-done.1 = bf16[4,80,256]{2,1,0:T(8,128)(2,1)S(1)} async-done(((bf16[4,80,256]{2,1,0:T(8,128)(2,1)}), bf16[4,80,256]{2,1,0:T(8,128)(2,1)S(1)}, u32[]{:S(2)}, u32[]{:S(2)}) %all-to-all-start.1) | async-done | bytes 163872 | tf_op jit(solution)/shard_map/all_to_all | solution.py:159
  16.0 3.5 %all-to-all-start = ((bf16[4,64,1024]{2,1,0:T(8,128)(2,1)}), bf16[4,64,1024]{2,1,0:T(8,128)(2,1)S(1)}, u32[]{:S(2)}, u32[]{:S(2)}) async-start(bf16[4,64,1024]{2,1,0:T(8,128)(2,1)} %bitcast.31), calls=%async_computation | async-start | bytes 1048576 | tf_op jit(solution)/shard_map/all_to_all | solution.py:176
  19.6 0.1 constant_dynamic-update-slice_fusion.refs_0_
  19.6 1.3 %collective-permute-start.3 = (bf16[272,256]{1,0:T(8,128)(2,1)S(1)}, bf16[272,256]{1,0:T(8,128)(2,1)S(1)}, u32[]{:S(2)}, u32[]{:S(2)}) collective-permute-start(bf16[272,256]{1,0:T(8,128)(2,1)S(1)} %constant_dynamic-update-slice_fusion.refs_0_), channel_id=1, source_target_pairs={{0,24},{4,28},{8,0},{12,4},{1,25},{5,29},{9,1},{13,5},{2,26},{6,30... | collective-permute-start | bytes 417800 | tf_op jit(solution)/shard_map/ppermute | solution.py:169
  20.9 1.3 %collective-permute-start.1 = (bf16[272,256]{1,0:T(8,128)(2,1)S(1)}, bf16[272,256]{1,0:T(8,128)(2,1)S(1)}, u32[]{:S(2)}, u32[]{:S(2)}) collective-permute-start(bf16[272,256]{1,0:T(8,128)(2,1)S(1)} %constant_dynamic-update-slice_fusion.refs_0_), channel_id=1, source_target_pairs={{0,8},{4,12},{8,16},{12,20},{16,24},{20,28},{1,9},{5,13},{9,17},{1... | collective-permute-start | bytes 417800 | tf_op jit(solution)/shard_map/ppermute | solution.py:167
  22.2 2.6 %collective-permute-start = (bf16[272,256]{1,0:T(8,128)(2,1)S(1)}, bf16[272,256]{1,0:T(8,128)(2,1)S(1)}, u32[]{:S(2)}, u32[]{:S(2)}) collective-permute-start(bf16[272,256]{1,0:T(8,128)(2,1)S(1)} %constant_dynamic-update-slice_fusion.refs_0_), channel_id=1, source_target_pairs={{0,4},{4,8},{8,12},{12,16},{16,20},{20,24},{24,28},{1,5},{5,9},{9,... | collective-permute-start | bytes 417800 | tf_op jit(solution)/shard_map/ppermute | solution.py:167
  24.8 6.0 %collective-permute-done.3 = bf16[272,256]{1,0:T(8,128)(2,1)S(1)} collective-permute-done((bf16[272,256]{1,0:T(8,128)(2,1)S(1)}, bf16[272,256]{1,0:T(8,128)(2,1)S(1)}, u32[]{:S(2)}, u32[]{:S(2)}) %collective-permute-start.3) | collective-permute-done | bytes 139296 | tf_op jit(solution)/shard_map/ppermute | solution.py:169
  30.8 1.9 %collective-permute-start.4 = (bf16[272,256]{1,0:T(8,128)(2,1)S(1)}, bf16[272,256]{1,0:T(8,128)(2,1)S(1)}, u32[]{:S(2)}, u32[]{:S(2)}) collective-permute-start(bf16[272,256]{1,0:T(8,128)(2,1)S(1)} %collective-permute-done.3), channel_id=1, source_target_pairs={{24,16},{28,20},{0,24},{4,28},{25,17},{29,21},{1,25},{5,29},{26,18... | collective-permute-start | bytes 417800 | tf_op jit(solution)/shard_map/ppermute | solution.py:172
  32.8 0.0 collective-permute-done.1.refs_2_
  32.8 1.9 %collective-permute-start.2 = (bf16[272,256]{1,0:T(8,128)(2,1)S(1)}, bf16[272,256]{1,0:T(8,128)(2,1)S(1)}, u32[]{:S(2)}, u32[]{:S(2)}) collective-permute-start(bf16[272,256]{1,0:T(8,128)(2,1)S(1)} %collective-permute-done.1.refs_2_), channel_id=1, source_target_pairs={{8,12},{12,16},{16,20},{20,24},{24,28},{9,13},{13,17},{17,21},{21,... | collective-permute-start | bytes 417800 | tf_op jit(solution)/shard_map/ppermute | solution.py:167
  34.7 0.0 collective-permute-done.refs_1_
  34.7 6.1 %collective-permute-done.4.refs_4_ = bf16[272,256]{1,0:T(8,128)(2,1)S(1)} collective-permute-done((bf16[272,256]{1,0:T(8,128)(2,1)S(1)}, bf16[272,256]{1,0:T(8,128)(2,1)S(1)}, u32[]{:S(2)}, u32[]{:S(2)}) %collective-permute-start.4) | collective-permute-done | bytes 139296 | tf_op jit(solution)/shard_map/ppermute | solution.py:172
  40.8 0.0 collective-permute-done.2.refs_3_
  40.9 0.0 all-to-all-done.q_ref
  40.9 4.2 %shard_map.60 = bf16[4,528,128]{2,1,0:T(8,128)(2,1)S(1)} custom-call(s32[1]{0:T(128)} %bitcast.row_ref, bf16[4,64,1024]{2,1,0:T(8,128)(2,1)S(1)} %all-to-all-done.q_ref, bf16[272,256]{1,0:T(8,128)(2,1)S(1)} %constant_dynamic-update-slice_fusion.refs_0_, bf16[272,256]{1,0:T(8,128)(2,1)S(1)} %collective-permute-done.refs_1_, ...), custom_call_target="tpu_custom_call" | custom-call | tf_op jit(solution)/shard_map/pallas_call | solution.py:119
  45.1 15.6 %all_to_all.15.in_ref = bf16[4,528,128]{2,1,0:T(8,128)(2,1)S(1)} all-to-all(bf16[4,528,128]{2,1,0:T(8,128)(2,1)S(1)} %shard_map.60), channel_id=1, replica_groups=mesh['grp'=16,'y'=8,'z'=4] {'z'}, dimensions={0} | all-to-all | bytes 1081344 | tf_op jit(solution)/shard_map/all_to_all | solution.py:178
  60.6 0.9 %shard_map.61 = (bf16[64,4096]{1,0:T(8,128)(2,1)}, f32[32,64]{1,0:T(8,128)}) custom-call(bf16[4,528,128]{2,1,0:T(8,128)(2,1)S(1)} %all_to_all.15.in_ref), custom_call_target="tpu_custom_call" | custom-call | tf_op jit(solution)/shard_map/pallas_call | solution.py:144
  (9 shorter events, 0.0 us)
Async XLA Ops:
  0.6 8.9 %copy-start = (bf16[64,4096]{1,0:T(8,128)(2,1)S(1)}, bf16[64,4096]{1,0:T(8,128)(2,1)}, u32[]{:S(2)}) copy-start(bf16[64,4096]{1,0:T(8,128)(2,1)} %param.4) | copy-start | bytes 1572868
  2.3 13.7 %all-to-all-start.1 = ((bf16[4,80,256]{2,1,0:T(8,128)(2,1)}), bf16[4,80,256]{2,1,0:T(8,128)(2,1)S(1)}, u32[]{:S(2)}, u32[]{:S(2)}) async-start(bf16[4,80,256]{2,1,0:T(8,128)(2,1)} %shard_map.59), calls=%async_computation.1 | async-start | bytes 327680 | tf_op jit(solution)/shard_map/all_to_all | solution.py:159
  16.0 24.9 %all-to-all-start = ((bf16[4,64,1024]{2,1,0:T(8,128)(2,1)}), bf16[4,64,1024]{2,1,0:T(8,128)(2,1)S(1)}, u32[]{:S(2)}, u32[]{:S(2)}) async-start(bf16[4,64,1024]{2,1,0:T(8,128)(2,1)} %bitcast.31), calls=%async_computation | async-start | bytes 1048576 | tf_op jit(solution)/shard_map/all_to_all | solution.py:176
  19.6 11.2 %collective-permute-start.3 = (bf16[272,256]{1,0:T(8,128)(2,1)S(1)}, bf16[272,256]{1,0:T(8,128)(2,1)S(1)}, u32[]{:S(2)}, u32[]{:S(2)}) collective-permute-start(bf16[272,256]{1,0:T(8,128)(2,1)S(1)} %constant_dynamic-update-slice_fusion.refs_0_), channel_id=1, source_target_pairs={{0,24},{4,28},{8,0},{12,4},{1,25},{5,29},{9,1},{13,5},{2,26},{6,30... | collective-permute-start | bytes 417800 | tf_op jit(solution)/shard_map/ppermute | solution.py:169
  20.9 11.8 %collective-permute-start.1 = (bf16[272,256]{1,0:T(8,128)(2,1)S(1)}, bf16[272,256]{1,0:T(8,128)(2,1)S(1)}, u32[]{:S(2)}, u32[]{:S(2)}) collective-permute-start(bf16[272,256]{1,0:T(8,128)(2,1)S(1)} %constant_dynamic-update-slice_fusion.refs_0_), channel_id=1, source_target_pairs={{0,8},{4,12},{8,16},{12,20},{16,24},{20,28},{1,9},{5,13},{9,17},{1... | collective-permute-start | bytes 417800 | tf_op jit(solution)/shard_map/ppermute | solution.py:167
  22.2 12.5 %collective-permute-start = (bf16[272,256]{1,0:T(8,128)(2,1)S(1)}, bf16[272,256]{1,0:T(8,128)(2,1)S(1)}, u32[]{:S(2)}, u32[]{:S(2)}) collective-permute-start(bf16[272,256]{1,0:T(8,128)(2,1)S(1)} %constant_dynamic-update-slice_fusion.refs_0_), channel_id=1, source_target_pairs={{0,4},{4,8},{8,12},{12,16},{16,20},{20,24},{24,28},{1,5},{5,9},{9,... | collective-permute-start | bytes 417800 | tf_op jit(solution)/shard_map/ppermute | solution.py:167
  30.8 10.0 %collective-permute-start.4 = (bf16[272,256]{1,0:T(8,128)(2,1)S(1)}, bf16[272,256]{1,0:T(8,128)(2,1)S(1)}, u32[]{:S(2)}, u32[]{:S(2)}) collective-permute-start(bf16[272,256]{1,0:T(8,128)(2,1)S(1)} %collective-permute-done.3), channel_id=1, source_target_pairs={{24,16},{28,20},{0,24},{4,28},{25,17},{29,21},{1,25},{5,29},{26,18... | collective-permute-start | bytes 417800 | tf_op jit(solution)/shard_map/ppermute | solution.py:172
  32.8 8.1 %collective-permute-start.2 = (bf16[272,256]{1,0:T(8,128)(2,1)S(1)}, bf16[272,256]{1,0:T(8,128)(2,1)S(1)}, u32[]{:S(2)}, u32[]{:S(2)}) collective-permute-start(bf16[272,256]{1,0:T(8,128)(2,1)S(1)} %collective-permute-done.1.refs_2_), channel_id=1, source_target_pairs={{8,12},{12,16},{16,20},{20,24},{24,28},{9,13},{13,17},{17,21},{21,... | collective-permute-start | bytes 417800 | tf_op jit(solution)/shard_map/ppermute | solution.py:167

commit v3 on v2

--- a/solution.py
+++ b/solution.py
@@ -15,6 +15,8 @@
 ROWS = 8
 COLS = 4
 NEG = -1e30
+SCALE = 1.0 / math.sqrt(DH)
+SCALE2 = SCALE * math.log2(math.e)
 VMEM = pl.BlockSpec(memory_space=pltpu.VMEM)
 SMEM = pl.BlockSpec(memory_space=pltpu.SMEM)
 ANY = pl.BlockSpec(memory_space=pl.ANY)
@@ -58,75 +60,153 @@
     )(key_rows, value_rows, doc_ids)
 
 
-def attend_kernel(row_ref, q_ref, *refs):
-    out_ref, bias_ref, value_ref = refs[-3:]
-    chunks = refs[:-3]
+def write_masks(row, own, chunks, bias_ref, value_ref):
+    tokens = bias_ref.shape[1]
+    doc_col = own[tokens:, :].astype(jnp.float32).T[:, :1]
+    for i, (back, chunk) in enumerate(chunks):
+        doc_row = chunk[tokens:, :].astype(jnp.float32)[:1]
+        allowed = doc_col == doc_row
+        if back == 0:
+            q_pos = lax.broadcasted_iota(jnp.int32, (tokens, tokens), 0)
+            k_pos = lax.broadcasted_iota(jnp.int32, (tokens, tokens), 1)
+            allowed = allowed & (k_pos <= q_pos)
+        else:
+            allowed = allowed & (row >= back)
+        bias_ref[i] = jnp.where(allowed, 0.0, NEG)
+        value_ref[i, :, :DH] = chunk[:tokens, DH:]
+        value_ref[i, :, DH:] = jnp.ones((tokens, DH), jnp.bfloat16)
+
+
+def masked_scores(q_ref, head, chunks, bias_ref):
+    tokens = bias_ref.shape[1]
+    query = q_ref[:, :, head * DH : (head + 1) * DH].reshape(tokens, DH)
+    scores = []
+    for i, (_, chunk) in enumerate(chunks):
+        product = lax.dot_general(
+            query, chunk[:tokens, :DH], (((1,), (1,)), ((), ())), preferred_element_type=jnp.float32
+        )
+        scores.append(product + bias_ref[i])
+    return scores, jnp.max(functools.reduce(jnp.maximum, scores), axis=1, keepdims=True)
+
+
+def weighted(scores, row_max, value_ref):
+    total = None
+    for i, score in enumerate(scores):
+        weights = jnp.exp2((score - row_max) * SCALE2).astype(jnp.bfloat16)
+        product = jnp.dot(weights, value_ref[i], preferred_element_type=jnp.float32)
+        total = product if total is None else total + product
+    return total
+
+
+def near_kernel(row_ref, q_ref, own_ref, first_ref, second_ref, sum_ref, max_ref, bias_ref, value_ref):
+    chunks = ((0, own_ref), (1, first_ref), (2, second_ref))
+    tokens = bias_ref.shape[1]
+    write_masks(row_ref[0], own_ref, chunks, bias_ref, value_ref)
+    for head in range(RATIO):
+        scores, row_max = masked_scores(q_ref, head, chunks, bias_ref)
+        sum_ref[head] = weighted(scores, row_max, value_ref)
+        max_ref[head] = jnp.broadcast_to(row_max, (tokens, DH))
+
+
+def far_kernel(row_ref, q_ref, own_ref, third_ref, fourth_ref, sum_ref, max_ref, out_ref, *scratch_refs):
+    bias_ref, value_ref, total_ref, top_ref = scratch_refs
+    chunks = ((3, third_ref), (4, fourth_ref))
     count = q_ref.shape[1]
     tokens = count * COLS
     row = row_ref[0]
-    doc_col = chunks[0][tokens:, :].astype(jnp.float32).T[:, :1]
-    q_pos = lax.broadcasted_iota(jnp.int32, (tokens, tokens), 0)
-    k_pos = lax.broadcasted_iota(jnp.int32, (tokens, tokens), 1)
-    for i, chunk in enumerate(chunks):
-        doc_row = chunk[tokens:, :].astype(jnp.float32)[:1]
-        allowed = doc_col == doc_row
-        if i == 0:
-            allowed = allowed & (k_pos <= q_pos)
-        else:
-            allowed = allowed & (row >= i)
-        bias_ref[i] = jnp.where(allowed, 0.0, NEG)
-        value_ref[i, :, :DH] = chunk[:tokens, DH:]
-        value_ref[i, :, DH:] = jnp.ones((tokens, DH), jnp.bfloat16)
-    scale = 1.0 / math.sqrt(DH)
-    scale2 = scale * math.log2(math.e)
+    last_doc = jnp.max(third_ref[tokens:, :].astype(jnp.float32))
+    first_doc = jnp.min(own_ref[tokens:, :].astype(jnp.float32))
+    wanted = (row >= 3) & (last_doc >= first_doc)
     lanes = lax.broadcasted_iota(jnp.int32, (tokens, DH), 1)
-    logs = jnp.zeros((tokens, DH), jnp.float32)
-    for head in range(RATIO):
-        part = slice(head * DH, (head + 1) * DH)
-        query = q_ref[:, :, part].reshape(tokens, DH)
-        scores = []
-        for i, chunk in enumerate(chunks):
-            product = lax.dot_general(
-                query,
-                chunk[:tokens, :DH],
-                (((1,), (1,)), ((), ())),
-                preferred_element_type=jnp.float32,
-            )
-            scores.append(product + bias_ref[i])
-        top = functools.reduce(jnp.maximum, scores)
-        row_max = jnp.max(top, axis=1, keepdims=True)
-        total = jnp.zeros((tokens, 2 * DH), jnp.float32)
-        for i in range(len(chunks)):
-            weights = jnp.exp2((scores[i] - row_max) * scale2).astype(jnp.bfloat16)
-            total += jnp.dot(weights, value_ref[i], preferred_element_type=jnp.float32)
+
+    def finish(head, total):
         denominator = total[:, DH:]
         mixed = (total[:, :DH] / denominator).astype(jnp.bfloat16)
         out_ref[:, head * count : (head + 1) * count, :] = mixed.reshape(COLS, count, DH)
-        log_total = row_max * scale + jnp.log(denominator)
-        high = log_total.astype(jnp.bfloat16).astype(jnp.float32)
-        logs = jnp.where(lanes == head, high, logs)
-        logs = jnp.where(lanes == RATIO + head, log_total - high, logs)
-    logs = logs.T[: 2 * RATIO]
+        return denominator
+
+    @pl.when(wanted)
+    def _():
+        write_masks(row, own_ref, chunks, bias_ref, value_ref)
+        tops = jnp.zeros((tokens, DH), jnp.float32)
+        sums = jnp.zeros((tokens, DH), jnp.float32)
+        for head in range(RATIO):
+            scores, row_max = masked_scores(q_ref, head, chunks, bias_ref)
+            near_max = max_ref[head]
+            row_max = jnp.maximum(near_max, row_max)
+            decay = jnp.exp2((near_max - row_max) * SCALE2)
+            total = sum_ref[head] * jnp.concatenate([decay, decay], 1)
+            wide_max = jnp.concatenate([row_max, row_max], 1)
+            denominator = finish(head, total + weighted(scores, wide_max, value_ref))
+            mine = lanes % RATIO == head
+            sums = jnp.where(mine, denominator, sums)
+            tops = jnp.where(mine, row_max, tops)
+        total_ref[...] = sums
+        top_ref[...] = tops
+
+    @pl.when(jnp.logical_not(wanted))
+    def _():
+        sums = jnp.zeros((tokens, DH), jnp.float32)
+        tops = jnp.zeros((tokens, DH), jnp.float32)
+        for head in range(RATIO):
+            mine = lanes % RATIO == head
+            sums = jnp.where(mine, finish(head, sum_ref[head]), sums)
+            tops = jnp.where(mine, max_ref[head], tops)
+        total_ref[...] = sums
+        top_ref[...] = tops
+
+    logs = top_ref[...] * SCALE + jnp.log(total_ref[...])
+    high = logs.astype(jnp.bfloat16).astype(jnp.float32)
+    logs = jnp.where(lanes < RATIO, high, logs - high).T[: 2 * RATIO]
     for step in range(COLS):
         piece = logs[:, step * count : (step + 1) * count]
         piece = jnp.concatenate([piece, piece], 1).astype(jnp.bfloat16)
         out_ref[step, RATIO * count :, :] = piece
 
 
-def attend(row, query, chunks):
+def cost(tokens, count):
+    return pl.CostEstimate(
+        flops=6 * RATIO * tokens * tokens * count * DH,
+        bytes_accessed=2 * 1024 * 1024,
+        transcendentals=RATIO * tokens * tokens * count,
+    )
+
+
+def scratch(count, tokens):
+    return [
+        pltpu.VMEM((count, tokens, tokens), jnp.float32),
+        pltpu.VMEM((count, tokens, 2 * DH), jnp.bfloat16),
+    ]
+
+
+def attend_near(row, query, own, first, second):
+    tokens = query.shape[1] * COLS
+    return pl.pallas_call(
+        near_kernel,
+        out_shape=[
+            jax.ShapeDtypeStruct((RATIO, tokens, 2 * DH), jnp.float32),
+            jax.ShapeDtypeStruct((RATIO, tokens, DH), jnp.float32),
+        ],
+        in_specs=[SMEM] + [VMEM] * 4,
+        out_specs=[VMEM] * 2,
+        scratch_shapes=scratch(3, tokens),
+        compiler_params=params(),
+        cost_estimate=cost(tokens, 3),
+    )(row, query, own, first, second)
+
+
+def attend_far(row, query, own, third, fourth, near):
     count = query.shape[1]
     tokens = count * COLS
     return pl.pallas_call(
-        attend_kernel,
+        far_kernel,
         out_shape=jax.ShapeDtypeStruct((COLS, RATIO * count + 2 * RATIO, DH), jnp.bfloat16),
-        in_specs=[SMEM] + [VMEM] * (1 + len(chunks)),
+        in_specs=[SMEM] + [VMEM] * 6,
         out_specs=VMEM,
-        scratch_shapes=[
-            pltpu.VMEM((len(chunks), tokens, tokens), jnp.float32),
-            pltpu.VMEM((len(chunks), tokens, 2 * DH), jnp.bfloat16),
-        ],
+        scratch_shapes=scratch(2, tokens) + [pltpu.VMEM((tokens, DH), jnp.float32)] * 2,
         compiler_params=params(),
-    )(row, query, *chunks)
+        cost_estimate=cost(tokens, 2),
+    )(row, query, own, third, fourth, *near)
 
 
 def join_kernel(in_ref, out_ref, log_ref):
@@ -174,7 +254,10 @@
 
     query = jnp.transpose(queries.reshape(count, COLS, RATIO * DH), (1, 0, 2))
     query = lax.all_to_all(query, "z", 0, 0, tiled=True)
-    blocks = attend(row.reshape(1), query, chunks)
+    own, first, second, third, fourth = chunks
+    row = row.reshape(1)
+    near = attend_near(row, query, own, first, second)
+    blocks = attend_far(row, query, own, third, fourth, near)
     blocks = lax.all_to_all(blocks, "z", 0, 0, tiled=True)
     attended, log_totals = join(blocks, count)
     return attended, log_totals

time: 61.9 us -> 60 us (0.969)
  waiting for transfers between devices: 17.7 us -> 14.1 us
  blocking collectives: 15.6 us -> 17.4 us
  Pallas kernels: 6.72 us -> 5.52 us
  local copies, waits for them, and re-layouts: 0.88 us -> 1.92 us
    ppermute x1, waiting for transfers between devices: 6.12 us -> 3.53 us  [per_device(): far = lax.ppermute(far, 'y', [((i + 6) % ROWS, i + 4) for i in range(4)])]
    all_to_all x1, blocking collectives: 15.6 us -> 17.4 us  [per_device(): blocks = lax.all_to_all(blocks, 'z', 0, 0, tiled=True)]
    pallas_call x1 -> x2, Pallas kernels: 4.2 us -> 3.04 us  [the longest x1 2.57 us: attend_near(): pl.pallas_call(near_kernel, out_shape=[jax.ShapeDtypeStruct((RATIO, token...]
    reshape x1, local copies, waits for them, and re-layouts: 0.83 us -> 1.87 us  [per_device(): query = jnp.transpose(queries.reshape(count, COLS, RATIO * DH), (1, 0, 2))]
    all_to_all x1, waiting for transfers between devices: 5.59 us -> 4.55 us  [per_device(): lax.all_to_all(pack(key_rows, value_rows, doc_ids), 'z', 0, 0, tiled=True)]
  transfers between devices with their start and end apart: 7 -> 7, of which waited for: 3 -> 3; matrix products, arithmetic and copies ran while one was open for 2% -> 3% of each run, Pallas kernels for 0% -> 4%
where the time goes in v3:
time: 60 us; the launch traced here: 59.5 us
  starting transfers between devices  19.8 us (33%)
  blocking collectives  17.4 us (29%)
  waiting for transfers between devices  14.1 us (24%)
  Pallas kernels  5.52 us (9%)
  local copies, waits for them, and re-layouts  1.92 us (3%)
  between operations  0.8 us (1%)
    all_to_all x1, blocking collectives, per_device(): blocks = lax.all_to_all(blocks, 'z', 0, 0, tiled=True)  17.4 us
    all_to_all x1, starting transfers between devices, per_device(): lax.all_to_all(pack(key_rows, value_rows, doc_ids), 'z', 0, 0, tiled=True)  7.27 us
    ppermute x1, waiting for transfers between devices, per_device(): far = lax.ppermute(own, 'y', [(i, (i + 6) % ROWS) for i in range(4)])  5.99 us
    ppermute x3, starting transfers between devices, ahead(): lax.ppermute(array, 'y', [(i, i + back) for i in range(least, ROWS - back)])  5.83 us
    all_to_all x1, waiting for transfers between devices, per_device(): lax.all_to_all(pack(key_rows, value_rows, doc_ids), 'z', 0, 0, tiled=True)  4.55 us
    ppermute x1, waiting for transfers between devices, per_device(): far = lax.ppermute(far, 'y', [((i + 6) % ROWS, i + 4) for i in range(4)])  3.53 us
    all_to_all x1, starting transfers between devices, per_device(): query = lax.all_to_all(query, 'z', 0, 0, tiled=True)  3.47 us
    pallas_call x1, Pallas kernels, attend_near(): pl.pallas_call(near_kernel, out_shape=[jax.ShapeDtypeStruct((RATIO, token...  2.57 us
  transfers between devices with their start and end apart: 7, of which 3 were waited for; matrix products, arithmetic and copies ran while one was open for 3% of the time, Pallas kernels for 4%

profile of v3, /device:TPU:48, one launch (start us, length us, event | category | flops | bytes accessed | tf_op | source)
XLA Modules:
  0.0 59.5 jit_solution(835580687012013164)
XLA Ops:
  0.6 1.6 %shard_map.59 = bf16[4,80,256]{2,1,0:T(8,128)(2,1)} custom-call(bf16[64,512]{1,0:T(8,128)(2,1)} %k_ref.1, bf16[64,512]{1,0:T(8,128)(2,1)} %v_ref.1, s32[1,64]{1,0:T(1,128)} %doc_ref.1), custom_call_target="tpu_custom_call" | custom-call | tf_op jit(solution)/shard_map/pallas_call | solution.py:50
  2.2 7.3 %all-to-all-start.1 = ((bf16[4,80,256]{2,1,0:T(8,128)(2,1)}), bf16[4,80,256]{2,1,0:T(8,128)(2,1)S(1)}, u32[]{:S(2)}, u32[]{:S(2)}) async-start(bf16[4,80,256]{2,1,0:T(8,128)(2,1)} %shard_map.59), calls=%async_computation.1 | async-start | bytes 327680 | tf_op jit(solution)/shard_map/all_to_all | solution.py:239
  9.5 1.9 %copy.9 = bf16[8,4,8,1024]{3,2,0,1:T(8,128)(2,1)} copy(bf16[8,4,8,1024]{3,2,1,0:T(8,128)(2,1)} %bitcast.32) | data formatting | bytes 1048576 | tf_op jit(solution)/shard_map/reshape | solution.py:255
  11.4 4.6 %all-to-all-done.1 = bf16[4,80,256]{2,1,0:T(8,128)(2,1)S(1)} async-done(((bf16[4,80,256]{2,1,0:T(8,128)(2,1)}), bf16[4,80,256]{2,1,0:T(8,128)(2,1)S(1)}, u32[]{:S(2)}, u32[]{:S(2)}) %all-to-all-start.1) | async-done | bytes 163872 | tf_op jit(solution)/shard_map/all_to_all | solution.py:239
  15.9 3.5 %all-to-all-start = ((bf16[4,64,1024]{2,1,0:T(8,128)(2,1)}), bf16[4,64,1024]{2,1,0:T(8,128)(2,1)S(1)}, u32[]{:S(2)}, u32[]{:S(2)}) async-start(bf16[4,64,1024]{2,1,0:T(8,128)(2,1)} %bitcast.31), calls=%async_computation | async-start | bytes 1048576 | tf_op jit(solution)/shard_map/all_to_all | solution.py:256
  19.5 0.1 constant_dynamic-update-slice_fusion.own_ref
  19.6 1.3 %collective-permute-start.2 = (bf16[272,256]{1,0:T(8,128)(2,1)S(1)}, bf16[272,256]{1,0:T(8,128)(2,1)S(1)}, u32[]{:S(2)}, u32[]{:S(2)}) collective-permute-start(bf16[272,256]{1,0:T(8,128)(2,1)S(1)} %constant_dynamic-update-slice_fusion.own_ref), channel_id=1, source_target_pairs={{0,24},{4,28},{8,0},{12,4},{1,25},{5,29},{9,1},{13,5},{2,26},{6,30... | collective-permute-start | bytes 417800 | tf_op jit(solution)/shard_map/ppermute | solution.py:249
  20.9 1.3 %collective-permute-start = (bf16[272,256]{1,0:T(8,128)(2,1)S(1)}, bf16[272,256]{1,0:T(8,128)(2,1)S(1)}, u32[]{:S(2)}, u32[]{:S(2)}) collective-permute-start(bf16[272,256]{1,0:T(8,128)(2,1)S(1)} %constant_dynamic-update-slice_fusion.own_ref), channel_id=1, source_target_pairs={{0,8},{4,12},{8,16},{12,20},{16,24},{20,28},{1,9},{5,13},{9,17},{1... | collective-permute-start | bytes 417800 | tf_op jit(solution)/shard_map/ppermute | solution.py:247
  22.2 2.6 %collective-permute-start.4 = (bf16[272,256]{1,0:T(8,128)(2,1)S(1)}, bf16[272,256]{1,0:T(8,128)(2,1)S(1)}, u32[]{:S(2)}, u32[]{:S(2)}) collective-permute-start(bf16[272,256]{1,0:T(8,128)(2,1)S(1)} %constant_dynamic-update-slice_fusion.own_ref), channel_id=1, source_target_pairs={{0,4},{4,8},{8,12},{12,16},{16,20},{20,24},{24,28},{1,5},{5,9},{9,... | collective-permute-start | bytes 417800 | tf_op jit(solution)/shard_map/ppermute | solution.py:247
  24.8 6.0 %collective-permute-done.2 = bf16[272,256]{1,0:T(8,128)(2,1)S(1)} collective-permute-done((bf16[272,256]{1,0:T(8,128)(2,1)S(1)}, bf16[272,256]{1,0:T(8,128)(2,1)S(1)}, u32[]{:S(2)}, u32[]{:S(2)}) %collective-permute-start.2) | collective-permute-done | bytes 139296 | tf_op jit(solution)/shard_map/ppermute | solution.py:249
  30.8 1.9 %collective-permute-start.3 = (bf16[272,256]{1,0:T(8,128)(2,1)S(1)}, bf16[272,256]{1,0:T(8,128)(2,1)S(1)}, u32[]{:S(2)}, u32[]{:S(2)}) collective-permute-start(bf16[272,256]{1,0:T(8,128)(2,1)S(1)} %collective-permute-done.2), channel_id=1, source_target_pairs={{24,16},{28,20},{0,24},{4,28},{25,17},{29,21},{1,25},{5,29},{26,18... | collective-permute-start | bytes 417800 | tf_op jit(solution)/shard_map/ppermute | solution.py:252
  32.7 0.0 collective-permute-done.second_ref
  32.7 2.0 %collective-permute-start.1 = (bf16[272,256]{1,0:T(8,128)(2,1)S(1)}, bf16[272,256]{1,0:T(8,128)(2,1)S(1)}, u32[]{:S(2)}, u32[]{:S(2)}) collective-permute-start(bf16[272,256]{1,0:T(8,128)(2,1)S(1)} %collective-permute-done.second_ref), channel_id=1, source_target_pairs={{8,12},{12,16},{16,20},{20,24},{24,28},{9,13},{13,17},{17,21},{21,... | collective-permute-start | bytes 417800 | tf_op jit(solution)/shard_map/ppermute | solution.py:247
  34.7 0.0 collective-permute-done.4.first_ref
  34.7 0.0 all-to-all-done.q_ref
  34.7 2.6 %shard_map.60 = (f32[8,256,256]{2,1,0:T(8,128)S(1)}, f32[8,256,128]{2,1,0:T(8,128)S(1)}) custom-call(s32[1]{0:T(128)} %bitcast.row_ref, bf16[4,64,1024]{2,1,0:T(8,128)(2,1)S(1)} %all-to-all-done.q_ref, bf16[272,256]{1,0:T(8,128)(2,1)S(1)} %constant_dynamic-update-slice_fusion.own_ref, bf16[272,256]{1,0:T(8,128)(2,1)S(1)} %collective-permute-done.4.first_ref, ...), custom_call_target="tpu_custom_call" | custom-call | flops 1207959552 | bytes 2097152 | tf_op jit(solution)/shard_map/pallas_call | solution.py:184
  37.3 3.5 %collective-permute-done.3.fourth_ref = bf16[272,256]{1,0:T(8,128)(2,1)S(1)} collective-permute-done((bf16[272,256]{1,0:T(8,128)(2,1)S(1)}, bf16[272,256]{1,0:T(8,128)(2,1)S(1)}, u32[]{:S(2)}, u32[]{:S(2)}) %collective-permute-start.3) | collective-permute-done | bytes 139296 | tf_op jit(solution)/shard_map/ppermute | solution.py:252
  40.8 0.0 collective-permute-done.1.third_ref
  40.8 0.5 shard_map.61
  41.3 17.4 %all_to_all.15.in_ref = bf16[4,528,128]{2,1,0:T(8,128)(2,1)S(1)} all-to-all(bf16[4,528,128]{2,1,0:T(8,128)(2,1)S(1)} %shard_map.61), channel_id=1, replica_groups=mesh['grp'=16,'y'=8,'z'=4] {'z'}, dimensions={0} | all-to-all | bytes 1081344 | tf_op jit(solution)/shard_map/all_to_all | solution.py:261
  58.6 0.9 %shard_map.62 = (bf16[64,4096]{1,0:T(8,128)(2,1)}, f32[32,64]{1,0:T(8,128)}) custom-call(bf16[4,528,128]{2,1,0:T(8,128)(2,1)S(1)} %all_to_all.15.in_ref), custom_call_target="tpu_custom_call" | custom-call | tf_op jit(solution)/shard_map/pallas_call | solution.py:224
  (9 shorter events, 0.0 us)
Async XLA Ops:
  2.2 13.7 %all-to-all-start.1 = ((bf16[4,80,256]{2,1,0:T(8,128)(2,1)}), bf16[4,80,256]{2,1,0:T(8,128)(2,1)S(1)}, u32[]{:S(2)}, u32[]{:S(2)}) async-start(bf16[4,80,256]{2,1,0:T(8,128)(2,1)} %shard_map.59), calls=%async_computation.1 | async-start | bytes 327680 | tf_op jit(solution)/shard_map/all_to_all | solution.py:239
  15.9 18.8 %all-to-all-start = ((bf16[4,64,1024]{2,1,0:T(8,128)(2,1)}), bf16[4,64,1024]{2,1,0:T(8,128)(2,1)S(1)}, u32[]{:S(2)}, u32[]{:S(2)}) async-start(bf16[4,64,1024]{2,1,0:T(8,128)(2,1)} %bitcast.31), calls=%async_computation | async-start | bytes 1048576 | tf_op jit(solution)/shard_map/all_to_all | solution.py:256
  19.6 11.2 %collective-permute-start.2 = (bf16[272,256]{1,0:T(8,128)(2,1)S(1)}, bf16[272,256]{1,0:T(8,128)(2,1)S(1)}, u32[]{:S(2)}, u32[]{:S(2)}) collective-permute-start(bf16[272,256]{1,0:T(8,128)(2,1)S(1)} %constant_dynamic-update-slice_fusion.own_ref), channel_id=1, source_target_pairs={{0,24},{4,28},{8,0},{12,4},{1,25},{5,29},{9,1},{13,5},{2,26},{6,30... | collective-permute-start | bytes 417800 | tf_op jit(solution)/shard_map/ppermute | solution.py:249
  20.9 11.8 %collective-permute-start = (bf16[272,256]{1,0:T(8,128)(2,1)S(1)}, bf16[272,256]{1,0:T(8,128)(2,1)S(1)}, u32[]{:S(2)}, u32[]{:S(2)}) collective-permute-start(bf16[272,256]{1,0:T(8,128)(2,1)S(1)} %constant_dynamic-update-slice_fusion.own_ref), channel_id=1, source_target_pairs={{0,8},{4,12},{8,16},{12,20},{16,24},{20,28},{1,9},{5,13},{9,17},{1... | collective-permute-start | bytes 417800 | tf_op jit(solution)/shard_map/ppermute | solution.py:247
  22.2 12.5 %collective-permute-start.4 = (bf16[272,256]{1,0:T(8,128)(2,1)S(1)}, bf16[272,256]{1,0:T(8,128)(2,1)S(1)}, u32[]{:S(2)}, u32[]{:S(2)}) collective-permute-start(bf16[272,256]{1,0:T(8,128)(2,1)S(1)} %constant_dynamic-update-slice_fusion.own_ref), channel_id=1, source_target_pairs={{0,4},{4,8},{8,12},{12,16},{16,20},{20,24},{24,28},{1,5},{5,9},{9,... | collective-permute-start | bytes 417800 | tf_op jit(solution)/shard_map/ppermute | solution.py:247
  30.8 10.0 %collective-permute-start.3 = (bf16[272,256]{1,0:T(8,128)(2,1)S(1)}, bf16[272,256]{1,0:T(8,128)(2,1)S(1)}, u32[]{:S(2)}, u32[]{:S(2)}) collective-permute-start(bf16[272,256]{1,0:T(8,128)(2,1)S(1)} %collective-permute-done.2), channel_id=1, source_target_pairs={{24,16},{28,20},{0,24},{4,28},{25,17},{29,21},{1,25},{5,29},{26,18... | collective-permute-start | bytes 417800 | tf_op jit(solution)/shard_map/ppermute | solution.py:252
  32.7 8.1 %collective-permute-start.1 = (bf16[272,256]{1,0:T(8,128)(2,1)S(1)}, bf16[272,256]{1,0:T(8,128)(2,1)S(1)}, u32[]{:S(2)}, u32[]{:S(2)}) collective-permute-start(bf16[272,256]{1,0:T(8,128)(2,1)S(1)} %collective-permute-done.second_ref), channel_id=1, source_target_pairs={{8,12},{12,16},{16,20},{20,24},{24,28},{9,13},{13,17},{17,21},{21,... | collective-permute-start | bytes 417800 | tf_op jit(solution)/shard_map/ppermute | solution.py:247

commit v4 on v3

--- a/solution.py
+++ b/solution.py
@@ -19,6 +19,7 @@
 SCALE2 = SCALE * math.log2(math.e)
 VMEM = pl.BlockSpec(memory_space=pltpu.VMEM)
 SMEM = pl.BlockSpec(memory_space=pltpu.SMEM)
+BACKWARD = [list(range(COLS))[::-1]]
 ANY = pl.BlockSpec(memory_space=pl.ANY)
 
 
@@ -122,7 +123,9 @@
     def finish(head, total):
         denominator = total[:, DH:]
         mixed = (total[:, :DH] / denominator).astype(jnp.bfloat16)
-        out_ref[:, head * count : (head + 1) * count, :] = mixed.reshape(COLS, count, DH)
+        for home in range(COLS):
+            piece = mixed[home * count : (home + 1) * count]
+            out_ref[COLS - 1 - home, head * count : (head + 1) * count, :] = piece
         return denominator
 
     @pl.when(wanted)
@@ -161,7 +164,7 @@
     for step in range(COLS):
         piece = logs[:, step * count : (step + 1) * count]
         piece = jnp.concatenate([piece, piece], 1).astype(jnp.bfloat16)
-        out_ref[step, RATIO * count :, :] = piece
+        out_ref[COLS - 1 - step, RATIO * count :, :] = piece
 
 
 def cost(tokens, count):
@@ -212,10 +215,11 @@
 def join_kernel(in_ref, out_ref, log_ref):
     count = out_ref.shape[0]
     for home in range(COLS):
+        block_ref = in_ref.at[COLS - 1 - home]
         for head in range(RATIO):
             first = (home * RATIO + head) * DH
-            out_ref[:, first : first + DH] = in_ref[home, head * count : (head + 1) * count, :]
-        logs = in_ref[home, RATIO * count :, :].astype(jnp.float32)
+            out_ref[:, first : first + DH] = block_ref[head * count : (head + 1) * count, :]
+        logs = block_ref[RATIO * count :, :].astype(jnp.float32)
         logs = logs[:RATIO] + logs[RATIO:]
         log_ref[home * RATIO : (home + 1) * RATIO, :] = logs[:, :count]
 
@@ -258,7 +262,7 @@
     row = row.reshape(1)
     near = attend_near(row, query, own, first, second)
     blocks = attend_far(row, query, own, third, fourth, near)
-    blocks = lax.all_to_all(blocks, "z", 0, 0, tiled=True)
+    blocks = lax.all_to_all(blocks, "z", 0, 0, tiled=True, axis_index_groups=BACKWARD)
     attended, log_totals = join(blocks, count)
     return attended, log_totals
 

time: 60 us -> 59.1 us (0.985)
  the two profiles are of different devices: /device:TPU:48 before, /device:TPU:54 now
where the time goes in v4:
time: 59.1 us; the launch traced here: 58.7 us
  starting transfers between devices  19.7 us (33%)
  blocking collectives  17.1 us (29%)
  waiting for transfers between devices  13.5 us (23%)
  Pallas kernels  5.52 us (9%)
  local copies, waits for them, and re-layouts  1.92 us (3%)
  between operations  0.8 us (1%)
    all_to_all x1, blocking collectives, per_device(): lax.all_to_all(blocks, 'z', 0, 0, tiled=True, axis_index_groups=BACKWARD)  17.1 us
    all_to_all x1, starting transfers between devices, per_device(): lax.all_to_all(pack(key_rows, value_rows, doc_ids), 'z', 0, 0, tiled=True)  7.27 us
    ppermute x1, waiting for transfers between devices, per_device(): far = lax.ppermute(own, 'y', [(i, (i + 6) % ROWS) for i in range(4)])  5.91 us
    ppermute x3, starting transfers between devices, ahead(): lax.ppermute(array, 'y', [(i, i + back) for i in range(least, ROWS - back)])  5.8 us
    all_to_all x1, waiting for transfers between devices, per_device(): lax.all_to_all(pack(key_rows, value_rows, doc_ids), 'z', 0, 0, tiled=True)  4.55 us
    all_to_all x1, starting transfers between devices, per_device(): query = lax.all_to_all(query, 'z', 0, 0, tiled=True)  3.47 us
    ppermute x1, waiting for transfers between devices, per_device(): far = lax.ppermute(far, 'y', [((i + 6) % ROWS, i + 4) for i in range(4)])  3.07 us
    pallas_call x1, Pallas kernels, attend_near(): pl.pallas_call(near_kernel, out_shape=[jax.ShapeDtypeStruct((RATIO, token...  2.57 us
  transfers between devices with their start and end apart: 7, of which 3 were waited for; matrix products, arithmetic and copies ran while one was open for 3% of the time, Pallas kernels for 4%

profile of v4, /device:TPU:54, one launch (start us, length us, event | category | flops | bytes accessed | tf_op | source)
XLA Modules:
  0.0 58.7 jit_solution(10132103182902107386)
XLA Ops:
  0.6 1.6 %shard_map.59 = bf16[4,80,256]{2,1,0:T(8,128)(2,1)} custom-call(bf16[64,512]{1,0:T(8,128)(2,1)} %k_ref.1, bf16[64,512]{1,0:T(8,128)(2,1)} %v_ref.1, s32[1,64]{1,0:T(1,128)} %doc_ref.1), custom_call_target="tpu_custom_call" | custom-call | tf_op jit(solution)/shard_map/pallas_call | solution.py:51
  2.2 7.3 %all-to-all-start.1 = ((bf16[4,80,256]{2,1,0:T(8,128)(2,1)}), bf16[4,80,256]{2,1,0:T(8,128)(2,1)S(1)}, u32[]{:S(2)}, u32[]{:S(2)}) async-start(bf16[4,80,256]{2,1,0:T(8,128)(2,1)} %shard_map.59), calls=%async_computation.1 | async-start | bytes 327680 | tf_op jit(solution)/shard_map/all_to_all | solution.py:243
  9.5 1.9 %copy.9 = bf16[8,4,8,1024]{3,2,0,1:T(8,128)(2,1)} copy(bf16[8,4,8,1024]{3,2,1,0:T(8,128)(2,1)} %bitcast.32) | data formatting | bytes 1048576 | tf_op jit(solution)/shard_map/reshape | solution.py:259
  11.4 4.6 %all-to-all-done.1 = bf16[4,80,256]{2,1,0:T(8,128)(2,1)S(1)} async-done(((bf16[4,80,256]{2,1,0:T(8,128)(2,1)}), bf16[4,80,256]{2,1,0:T(8,128)(2,1)S(1)}, u32[]{:S(2)}, u32[]{:S(2)}) %all-to-all-start.1) | async-done | bytes 163872 | tf_op jit(solution)/shard_map/all_to_all | solution.py:243
  15.9 3.5 %all-to-all-start = ((bf16[4,64,1024]{2,1,0:T(8,128)(2,1)}), bf16[4,64,1024]{2,1,0:T(8,128)(2,1)S(1)}, u32[]{:S(2)}, u32[]{:S(2)}) async-start(bf16[4,64,1024]{2,1,0:T(8,128)(2,1)} %bitcast.31), calls=%async_computation | async-start | bytes 1048576 | tf_op jit(solution)/shard_map/all_to_all | solution.py:260
  19.5 0.1 constant_dynamic-update-slice_fusion.own_ref
  19.6 1.3 %collective-permute-start.2 = (bf16[272,256]{1,0:T(8,128)(2,1)S(1)}, bf16[272,256]{1,0:T(8,128)(2,1)S(1)}, u32[]{:S(2)}, u32[]{:S(2)}) collective-permute-start(bf16[272,256]{1,0:T(8,128)(2,1)S(1)} %constant_dynamic-update-slice_fusion.own_ref), channel_id=1, source_target_pairs={{0,24},{4,28},{8,0},{12,4},{1,25},{5,29},{9,1},{13,5},{2,26},{6,30... | collective-permute-start | bytes 417800 | tf_op jit(solution)/shard_map/ppermute | solution.py:253
  20.9 1.3 %collective-permute-start = (bf16[272,256]{1,0:T(8,128)(2,1)S(1)}, bf16[272,256]{1,0:T(8,128)(2,1)S(1)}, u32[]{:S(2)}, u32[]{:S(2)}) collective-permute-start(bf16[272,256]{1,0:T(8,128)(2,1)S(1)} %constant_dynamic-update-slice_fusion.own_ref), channel_id=1, source_target_pairs={{0,8},{4,12},{8,16},{12,20},{16,24},{20,28},{1,9},{5,13},{9,17},{1... | collective-permute-start | bytes 417800 | tf_op jit(solution)/shard_map/ppermute | solution.py:251
  22.2 2.6 %collective-permute-start.4 = (bf16[272,256]{1,0:T(8,128)(2,1)S(1)}, bf16[272,256]{1,0:T(8,128)(2,1)S(1)}, u32[]{:S(2)}, u32[]{:S(2)}) collective-permute-start(bf16[272,256]{1,0:T(8,128)(2,1)S(1)} %constant_dynamic-update-slice_fusion.own_ref), channel_id=1, source_target_pairs={{0,4},{4,8},{8,12},{12,16},{16,20},{20,24},{24,28},{1,5},{5,9},{9,... | collective-permute-start | bytes 417800 | tf_op jit(solution)/shard_map/ppermute | solution.py:251
  24.8 5.9 %collective-permute-done.2 = bf16[272,256]{1,0:T(8,128)(2,1)S(1)} collective-permute-done((bf16[272,256]{1,0:T(8,128)(2,1)S(1)}, bf16[272,256]{1,0:T(8,128)(2,1)S(1)}, u32[]{:S(2)}, u32[]{:S(2)}) %collective-permute-start.2) | collective-permute-done | bytes 139296 | tf_op jit(solution)/shard_map/ppermute | solution.py:253
  30.7 1.9 %collective-permute-start.3 = (bf16[272,256]{1,0:T(8,128)(2,1)S(1)}, bf16[272,256]{1,0:T(8,128)(2,1)S(1)}, u32[]{:S(2)}, u32[]{:S(2)}) collective-permute-start(bf16[272,256]{1,0:T(8,128)(2,1)S(1)} %collective-permute-done.2), channel_id=1, source_target_pairs={{24,16},{28,20},{0,24},{4,28},{25,17},{29,21},{1,25},{5,29},{26,18... | collective-permute-start | bytes 417800 | tf_op jit(solution)/shard_map/ppermute | solution.py:256
  32.6 0.0 collective-permute-done.second_ref
  32.6 1.9 %collective-permute-start.1 = (bf16[272,256]{1,0:T(8,128)(2,1)S(1)}, bf16[272,256]{1,0:T(8,128)(2,1)S(1)}, u32[]{:S(2)}, u32[]{:S(2)}) collective-permute-start(bf16[272,256]{1,0:T(8,128)(2,1)S(1)} %collective-permute-done.second_ref), channel_id=1, source_target_pairs={{8,12},{12,16},{16,20},{20,24},{24,28},{9,13},{13,17},{17,21},{21,... | collective-permute-start | bytes 417800 | tf_op jit(solution)/shard_map/ppermute | solution.py:251
  34.5 0.0 collective-permute-done.4.first_ref
  34.6 0.0 all-to-all-done.q_ref
  34.6 2.6 %shard_map.60 = (f32[8,256,256]{2,1,0:T(8,128)S(1)}, f32[8,256,128]{2,1,0:T(8,128)S(1)}) custom-call(s32[1]{0:T(128)} %bitcast.row_ref, bf16[4,64,1024]{2,1,0:T(8,128)(2,1)S(1)} %all-to-all-done.q_ref, bf16[272,256]{1,0:T(8,128)(2,1)S(1)} %constant_dynamic-update-slice_fusion.own_ref, bf16[272,256]{1,0:T(8,128)(2,1)S(1)} %collective-permute-done.4.first_ref, ...), custom_call_target="tpu_custom_call" | custom-call | flops 1207959552 | bytes 2097152 | tf_op jit(solution)/shard_map/pallas_call | solution.py:187
  37.1 3.1 %collective-permute-done.3.fourth_ref = bf16[272,256]{1,0:T(8,128)(2,1)S(1)} collective-permute-done((bf16[272,256]{1,0:T(8,128)(2,1)S(1)}, bf16[272,256]{1,0:T(8,128)(2,1)S(1)}, u32[]{:S(2)}, u32[]{:S(2)}) %collective-permute-start.3) | collective-permute-done | bytes 139296 | tf_op jit(solution)/shard_map/ppermute | solution.py:256
  40.2 0.0 collective-permute-done.1.third_ref
  40.2 0.5 shard_map.61
  40.7 17.1 %all_to_all.15.in_ref = bf16[4,528,128]{2,1,0:T(8,128)(2,1)S(1)} all-to-all(bf16[4,528,128]{2,1,0:T(8,128)(2,1)S(1)} %shard_map.61), channel_id=1, replica_groups={{3,2,1,0},{7,6,5,4},{11,10,9,8},{15,14,13,12},{19,18,17,16},{23,22,21,2..., dimensions={0} | all-to-all | bytes 1081344 | tf_op jit(solution)/shard_map/all_to_all | solution.py:265
  57.8 0.9 %shard_map.62 = (bf16[64,4096]{1,0:T(8,128)(2,1)}, f32[32,64]{1,0:T(8,128)}) custom-call(bf16[4,528,128]{2,1,0:T(8,128)(2,1)S(1)} %all_to_all.15.in_ref), custom_call_target="tpu_custom_call" | custom-call | tf_op jit(solution)/shard_map/pallas_call | solution.py:228
  (9 shorter events, 0.0 us)
Async XLA Ops:
  2.2 13.7 %all-to-all-start.1 = ((bf16[4,80,256]{2,1,0:T(8,128)(2,1)}), bf16[4,80,256]{2,1,0:T(8,128)(2,1)S(1)}, u32[]{:S(2)}, u32[]{:S(2)}) async-start(bf16[4,80,256]{2,1,0:T(8,128)(2,1)} %shard_map.59), calls=%async_computation.1 | async-start | bytes 327680 | tf_op jit(solution)/shard_map/all_to_all | solution.py:243
  15.9 18.6 %all-to-all-start = ((bf16[4,64,1024]{2,1,0:T(8,128)(2,1)}), bf16[4,64,1024]{2,1,0:T(8,128)(2,1)S(1)}, u32[]{:S(2)}, u32[]{:S(2)}) async-start(bf16[4,64,1024]{2,1,0:T(8,128)(2,1)} %bitcast.31), calls=%async_computation | async-start | bytes 1048576 | tf_op jit(solution)/shard_map/all_to_all | solution.py:260
  19.6 11.1 %collective-permute-start.2 = (bf16[272,256]{1,0:T(8,128)(2,1)S(1)}, bf16[272,256]{1,0:T(8,128)(2,1)S(1)}, u32[]{:S(2)}, u32[]{:S(2)}) collective-permute-start(bf16[272,256]{1,0:T(8,128)(2,1)S(1)} %constant_dynamic-update-slice_fusion.own_ref), channel_id=1, source_target_pairs={{0,24},{4,28},{8,0},{12,4},{1,25},{5,29},{9,1},{13,5},{2,26},{6,30... | collective-permute-start | bytes 417800 | tf_op jit(solution)/shard_map/ppermute | solution.py:253
  20.9 11.7 %collective-permute-start = (bf16[272,256]{1,0:T(8,128)(2,1)S(1)}, bf16[272,256]{1,0:T(8,128)(2,1)S(1)}, u32[]{:S(2)}, u32[]{:S(2)}) collective-permute-start(bf16[272,256]{1,0:T(8,128)(2,1)S(1)} %constant_dynamic-update-slice_fusion.own_ref), channel_id=1, source_target_pairs={{0,8},{4,12},{8,16},{12,20},{16,24},{20,28},{1,9},{5,13},{9,17},{1... | collective-permute-start | bytes 417800 | tf_op jit(solution)/shard_map/ppermute | solution.py:251
  22.2 12.4 %collective-permute-start.4 = (bf16[272,256]{1,0:T(8,128)(2,1)S(1)}, bf16[272,256]{1,0:T(8,128)(2,1)S(1)}, u32[]{:S(2)}, u32[]{:S(2)}) collective-permute-start(bf16[272,256]{1,0:T(8,128)(2,1)S(1)} %constant_dynamic-update-slice_fusion.own_ref), channel_id=1, source_target_pairs={{0,4},{4,8},{8,12},{12,16},{16,20},{20,24},{24,28},{1,5},{5,9},{9,... | collective-permute-start | bytes 417800 | tf_op jit(solution)/shard_map/ppermute | solution.py:251
  30.7 9.5 %collective-permute-start.3 = (bf16[272,256]{1,0:T(8,128)(2,1)S(1)}, bf16[272,256]{1,0:T(8,128)(2,1)S(1)}, u32[]{:S(2)}, u32[]{:S(2)}) collective-permute-start(bf16[272,256]{1,0:T(8,128)(2,1)S(1)} %collective-permute-done.2), channel_id=1, source_target_pairs={{24,16},{28,20},{0,24},{4,28},{25,17},{29,21},{1,25},{5,29},{26,18... | collective-permute-start | bytes 417800 | tf_op jit(solution)/shard_map/ppermute | solution.py:256
  32.6 7.6 %collective-permute-start.1 = (bf16[272,256]{1,0:T(8,128)(2,1)S(1)}, bf16[272,256]{1,0:T(8,128)(2,1)S(1)}, u32[]{:S(2)}, u32[]{:S(2)}) collective-permute-start(bf16[272,256]{1,0:T(8,128)(2,1)S(1)} %collective-permute-done.second_ref), channel_id=1, source_target_pairs={{8,12},{12,16},{16,20},{20,24},{24,28},{9,13},{13,17},{17,21},{21,... | collective-permute-start | bytes 417800 | tf_op jit(solution)/shard_map/ppermute | solution.py:251

commit v5 on v4

--- a/solution.py
+++ b/solution.py
@@ -19,7 +19,7 @@
 SCALE2 = SCALE * math.log2(math.e)
 VMEM = pl.BlockSpec(memory_space=pltpu.VMEM)
 SMEM = pl.BlockSpec(memory_space=pltpu.SMEM)
-BACKWARD = [list(range(COLS))[::-1]]
+ORDER = (2, 3, 1, 0)
 ANY = pl.BlockSpec(memory_space=pl.ANY)
 
 
@@ -125,7 +125,7 @@
         mixed = (total[:, :DH] / denominator).astype(jnp.bfloat16)
         for home in range(COLS):
             piece = mixed[home * count : (home + 1) * count]
-            out_ref[COLS - 1 - home, head * count : (head + 1) * count, :] = piece
+            out_ref[ORDER.index(home), head * count : (head + 1) * count, :] = piece
         return denominator
 
     @pl.when(wanted)
@@ -164,7 +164,7 @@
     for step in range(COLS):
         piece = logs[:, step * count : (step + 1) * count]
         piece = jnp.concatenate([piece, piece], 1).astype(jnp.bfloat16)
-        out_ref[COLS - 1 - step, RATIO * count :, :] = piece
+        out_ref[ORDER.index(step), RATIO * count :, :] = piece
 
 
 def cost(tokens, count):
@@ -215,7 +215,7 @@
 def join_kernel(in_ref, out_ref, log_ref):
     count = out_ref.shape[0]
     for home in range(COLS):
-        block_ref = in_ref.at[COLS - 1 - home]
+        block_ref = in_ref.at[ORDER.index(home)]
         for head in range(RATIO):
             first = (home * RATIO + head) * DH
             out_ref[:, first : first + DH] = block_ref[head * count : (head + 1) * count, :]
@@ -262,7 +262,7 @@
     row = row.reshape(1)
     near = attend_near(row, query, own, first, second)
     blocks = attend_far(row, query, own, third, fourth, near)
-    blocks = lax.all_to_all(blocks, "z", 0, 0, tiled=True, axis_index_groups=BACKWARD)
+    blocks = lax.all_to_all(blocks, "z", 0, 0, tiled=True, axis_index_groups=[list(ORDER)])
     attended, log_totals = join(blocks, count)
     return attended, log_totals
 

time: 59.1 us -> 58 us (0.981)
  the two profiles are of different devices: /device:TPU:54 before, /device:TPU:48 now
where the time goes in v5:
time: 58 us; the launch traced here: 57.5 us
  starting transfers between devices  19.8 us (34%)
  waiting for transfers between devices  14.1 us (24%)
  blocking collectives  13.6 us (23%)
  Pallas kernels  7.32 us (13%)
  local copies, waits for them, and re-layouts  1.92 us (3%)
  between operations  0.8 us (1%)
    all_to_all x1, blocking collectives, per_device(): lax.all_to_all(blocks, 'z', 0, 0, tiled=True, axis_index_groups=[list(ORD...  13.6 us
    all_to_all x1, starting transfers between devices, per_device(): lax.all_to_all(pack(key_rows, value_rows, doc_ids), 'z', 0, 0, tiled=True)  7.27 us
    ppermute x1, waiting for transfers between devices, per_device(): far = lax.ppermute(own, 'y', [(i, (i + 6) % ROWS) for i in range(4)])  5.99 us
    ppermute x3, starting transfers between devices, ahead(): lax.ppermute(array, 'y', [(i, i + back) for i in range(least, ROWS - back)])  5.83 us
    all_to_all x1, waiting for transfers between devices, per_device(): lax.all_to_all(pack(key_rows, value_rows, doc_ids), 'z', 0, 0, tiled=True)  4.55 us
    ppermute x1, waiting for transfers between devices, per_device(): far = lax.ppermute(far, 'y', [((i + 6) % ROWS, i + 4) for i in range(4)])  3.53 us
    all_to_all x1, starting transfers between devices, per_device(): query = lax.all_to_all(query, 'z', 0, 0, tiled=True)  3.47 us
    pallas_call x1, Pallas kernels, attend_near(): pl.pallas_call(near_kernel, out_shape=[jax.ShapeDtypeStruct((RATIO, token...  2.57 us
  transfers between devices with their start and end apart: 7, of which 3 were waited for; matrix products, arithmetic and copies ran while one was open for 3% of the time, Pallas kernels for 4%

profile of v5, /device:TPU:48, one launch (start us, length us, event | category | flops | bytes accessed | tf_op | source)
XLA Modules:
  0.0 57.5 jit_solution(203950376532099823)
XLA Ops:
  0.6 1.6 %shard_map.59 = bf16[4,80,256]{2,1,0:T(8,128)(2,1)} custom-call(bf16[64,512]{1,0:T(8,128)(2,1)} %k_ref.1, bf16[64,512]{1,0:T(8,128)(2,1)} %v_ref.1, s32[1,64]{1,0:T(1,128)} %doc_ref.1), custom_call_target="tpu_custom_call" | custom-call | tf_op jit(solution)/shard_map/pallas_call | solution.py:51
  2.2 7.3 %all-to-all-start.1 = ((bf16[4,80,256]{2,1,0:T(8,128)(2,1)}), bf16[4,80,256]{2,1,0:T(8,128)(2,1)S(1)}, u32[]{:S(2)}, u32[]{:S(2)}) async-start(bf16[4,80,256]{2,1,0:T(8,128)(2,1)} %shard_map.59), calls=%async_computation.1 | async-start | bytes 327680 | tf_op jit(solution)/shard_map/all_to_all | solution.py:243
  9.5 1.9 %copy.9 = bf16[8,4,8,1024]{3,2,0,1:T(8,128)(2,1)} copy(bf16[8,4,8,1024]{3,2,1,0:T(8,128)(2,1)} %bitcast.32) | data formatting | bytes 1048576 | tf_op jit(solution)/shard_map/reshape | solution.py:259
  11.4 4.6 %all-to-all-done.1 = bf16[4,80,256]{2,1,0:T(8,128)(2,1)S(1)} async-done(((bf16[4,80,256]{2,1,0:T(8,128)(2,1)}), bf16[4,80,256]{2,1,0:T(8,128)(2,1)S(1)}, u32[]{:S(2)}, u32[]{:S(2)}) %all-to-all-start.1) | async-done | bytes 163872 | tf_op jit(solution)/shard_map/all_to_all | solution.py:243
  15.9 3.5 %all-to-all-start = ((bf16[4,64,1024]{2,1,0:T(8,128)(2,1)}), bf16[4,64,1024]{2,1,0:T(8,128)(2,1)S(1)}, u32[]{:S(2)}, u32[]{:S(2)}) async-start(bf16[4,64,1024]{2,1,0:T(8,128)(2,1)} %bitcast.31), calls=%async_computation | async-start | bytes 1048576 | tf_op jit(solution)/shard_map/all_to_all | solution.py:260
  19.5 0.1 constant_dynamic-update-slice_fusion.own_ref
  19.6 1.3 %collective-permute-start.2 = (bf16[272,256]{1,0:T(8,128)(2,1)S(1)}, bf16[272,256]{1,0:T(8,128)(2,1)S(1)}, u32[]{:S(2)}, u32[]{:S(2)}) collective-permute-start(bf16[272,256]{1,0:T(8,128)(2,1)S(1)} %constant_dynamic-update-slice_fusion.own_ref), channel_id=1, source_target_pairs={{0,24},{4,28},{8,0},{12,4},{1,25},{5,29},{9,1},{13,5},{2,26},{6,30... | collective-permute-start | bytes 417800 | tf_op jit(solution)/shard_map/ppermute | solution.py:253
  20.9 1.3 %collective-permute-start = (bf16[272,256]{1,0:T(8,128)(2,1)S(1)}, bf16[272,256]{1,0:T(8,128)(2,1)S(1)}, u32[]{:S(2)}, u32[]{:S(2)}) collective-permute-start(bf16[272,256]{1,0:T(8,128)(2,1)S(1)} %constant_dynamic-update-slice_fusion.own_ref), channel_id=1, source_target_pairs={{0,8},{4,12},{8,16},{12,20},{16,24},{20,28},{1,9},{5,13},{9,17},{1... | collective-permute-start | bytes 417800 | tf_op jit(solution)/shard_map/ppermute | solution.py:251
  22.2 2.6 %collective-permute-start.4 = (bf16[272,256]{1,0:T(8,128)(2,1)S(1)}, bf16[272,256]{1,0:T(8,128)(2,1)S(1)}, u32[]{:S(2)}, u32[]{:S(2)}) collective-permute-start(bf16[272,256]{1,0:T(8,128)(2,1)S(1)} %constant_dynamic-update-slice_fusion.own_ref), channel_id=1, source_target_pairs={{0,4},{4,8},{8,12},{12,16},{16,20},{20,24},{24,28},{1,5},{5,9},{9,... | collective-permute-start | bytes 417800 | tf_op jit(solution)/shard_map/ppermute | solution.py:251
  24.8 6.0 %collective-permute-done.2 = bf16[272,256]{1,0:T(8,128)(2,1)S(1)} collective-permute-done((bf16[272,256]{1,0:T(8,128)(2,1)S(1)}, bf16[272,256]{1,0:T(8,128)(2,1)S(1)}, u32[]{:S(2)}, u32[]{:S(2)}) %collective-permute-start.2) | collective-permute-done | bytes 139296 | tf_op jit(solution)/shard_map/ppermute | solution.py:253
  30.8 1.9 %collective-permute-start.3 = (bf16[272,256]{1,0:T(8,128)(2,1)S(1)}, bf16[272,256]{1,0:T(8,128)(2,1)S(1)}, u32[]{:S(2)}, u32[]{:S(2)}) collective-permute-start(bf16[272,256]{1,0:T(8,128)(2,1)S(1)} %collective-permute-done.2), channel_id=1, source_target_pairs={{24,16},{28,20},{0,24},{4,28},{25,17},{29,21},{1,25},{5,29},{26,18... | collective-permute-start | bytes 417800 | tf_op jit(solution)/shard_map/ppermute | solution.py:256
  32.7 0.0 collective-permute-done.second_ref
  32.7 2.0 %collective-permute-start.1 = (bf16[272,256]{1,0:T(8,128)(2,1)S(1)}, bf16[272,256]{1,0:T(8,128)(2,1)S(1)}, u32[]{:S(2)}, u32[]{:S(2)}) collective-permute-start(bf16[272,256]{1,0:T(8,128)(2,1)S(1)} %collective-permute-done.second_ref), channel_id=1, source_target_pairs={{8,12},{12,16},{16,20},{20,24},{24,28},{9,13},{13,17},{17,21},{21,... | collective-permute-start | bytes 417800 | tf_op jit(solution)/shard_map/ppermute | solution.py:251
  34.7 0.0 collective-permute-done.4.first_ref
  34.7 0.0 all-to-all-done.q_ref
  34.7 2.6 %shard_map.60 = (f32[8,256,256]{2,1,0:T(8,128)S(1)}, f32[8,256,128]{2,1,0:T(8,128)S(1)}) custom-call(s32[1]{0:T(128)} %bitcast.row_ref, bf16[4,64,1024]{2,1,0:T(8,128)(2,1)S(1)} %all-to-all-done.q_ref, bf16[272,256]{1,0:T(8,128)(2,1)S(1)} %constant_dynamic-update-slice_fusion.own_ref, bf16[272,256]{1,0:T(8,128)(2,1)S(1)} %collective-permute-done.4.first_ref, ...), custom_call_target="tpu_custom_call" | custom-call | flops 1207959552 | bytes 2097152 | tf_op jit(solution)/shard_map/pallas_call | solution.py:187
  37.3 3.5 %collective-permute-done.3.fourth_ref = bf16[272,256]{1,0:T(8,128)(2,1)S(1)} collective-permute-done((bf16[272,256]{1,0:T(8,128)(2,1)S(1)}, bf16[272,256]{1,0:T(8,128)(2,1)S(1)}, u32[]{:S(2)}, u32[]{:S(2)}) %collective-permute-start.3) | collective-permute-done | bytes 139296 | tf_op jit(solution)/shard_map/ppermute | solution.py:256
  40.8 0.0 collective-permute-done.1.third_ref
  40.8 2.3 %shard_map.61 = bf16[4,528,128]{2,1,0:T(8,128)(2,1)S(1)} custom-call(s32[1]{0:T(128)} %bitcast.row_ref, bf16[4,64,1024]{2,1,0:T(8,128)(2,1)S(1)} %all-to-all-done.q_ref, bf16[272,256]{1,0:T(8,128)(2,1)S(1)} %constant_dynamic-update-slice_fusion.own_ref, bf16[272,256]{1,0:T(8,128)(2,1)S(1)} %collective-permute-done.1.third_ref, ...), custom_call_target="tpu_custom_call" | custom-call | flops 805306368 | bytes 2097152 | tf_op jit(solution)/shard_map/pallas_call | solution.py:204
  43.1 13.6 %all_to_all.15.in_ref = bf16[4,528,128]{2,1,0:T(8,128)(2,1)S(1)} all-to-all(bf16[4,528,128]{2,1,0:T(8,128)(2,1)S(1)} %shard_map.61), channel_id=1, replica_groups={{2,3,1,0},{6,7,5,4},{10,11,9,8},{14,15,13,12},{18,19,17,16},{22,23,21,2..., dimensions={0} | all-to-all | bytes 1081344 | tf_op jit(solution)/shard_map/all_to_all | solution.py:265
  56.7 0.9 %shard_map.62 = (bf16[64,4096]{1,0:T(8,128)(2,1)}, f32[32,64]{1,0:T(8,128)}) custom-call(bf16[4,528,128]{2,1,0:T(8,128)(2,1)S(1)} %all_to_all.15.in_ref), custom_call_target="tpu_custom_call" | custom-call | tf_op jit(solution)/shard_map/pallas_call | solution.py:228
  (9 shorter events, 0.0 us)
Async XLA Ops:
  2.2 13.7 %all-to-all-start.1 = ((bf16[4,80,256]{2,1,0:T(8,128)(2,1)}), bf16[4,80,256]{2,1,0:T(8,128)(2,1)S(1)}, u32[]{:S(2)}, u32[]{:S(2)}) async-start(bf16[4,80,256]{2,1,0:T(8,128)(2,1)} %shard_map.59), calls=%async_computation.1 | async-start | bytes 327680 | tf_op jit(solution)/shard_map/all_to_all | solution.py:243
  15.9 18.8 %all-to-all-start = ((bf16[4,64,1024]{2,1,0:T(8,128)(2,1)}), bf16[4,64,1024]{2,1,0:T(8,128)(2,1)S(1)}, u32[]{:S(2)}, u32[]{:S(2)}) async-start(bf16[4,64,1024]{2,1,0:T(8,128)(2,1)} %bitcast.31), calls=%async_computation | async-start | bytes 1048576 | tf_op jit(solution)/shard_map/all_to_all | solution.py:260
  19.6 11.2 %collective-permute-start.2 = (bf16[272,256]{1,0:T(8,128)(2,1)S(1)}, bf16[272,256]{1,0:T(8,128)(2,1)S(1)}, u32[]{:S(2)}, u32[]{:S(2)}) collective-permute-start(bf16[272,256]{1,0:T(8,128)(2,1)S(1)} %constant_dynamic-update-slice_fusion.own_ref), channel_id=1, source_target_pairs={{0,24},{4,28},{8,0},{12,4},{1,25},{5,29},{9,1},{13,5},{2,26},{6,30... | collective-permute-start | bytes 417800 | tf_op jit(solution)/shard_map/ppermute | solution.py:253
  20.9 11.8 %collective-permute-start = (bf16[272,256]{1,0:T(8,128)(2,1)S(1)}, bf16[272,256]{1,0:T(8,128)(2,1)S(1)}, u32[]{:S(2)}, u32[]{:S(2)}) collective-permute-start(bf16[272,256]{1,0:T(8,128)(2,1)S(1)} %constant_dynamic-update-slice_fusion.own_ref), channel_id=1, source_target_pairs={{0,8},{4,12},{8,16},{12,20},{16,24},{20,28},{1,9},{5,13},{9,17},{1... | collective-permute-start | bytes 417800 | tf_op jit(solution)/shard_map/ppermute | solution.py:251
  22.2 12.5 %collective-permute-start.4 = (bf16[272,256]{1,0:T(8,128)(2,1)S(1)}, bf16[272,256]{1,0:T(8,128)(2,1)S(1)}, u32[]{:S(2)}, u32[]{:S(2)}) collective-permute-start(bf16[272,256]{1,0:T(8,128)(2,1)S(1)} %constant_dynamic-update-slice_fusion.own_ref), channel_id=1, source_target_pairs={{0,4},{4,8},{8,12},{12,16},{16,20},{20,24},{24,28},{1,5},{5,9},{9,... | collective-permute-start | bytes 417800 | tf_op jit(solution)/shard_map/ppermute | solution.py:251
  30.8 10.0 %collective-permute-start.3 = (bf16[272,256]{1,0:T(8,128)(2,1)S(1)}, bf16[272,256]{1,0:T(8,128)(2,1)S(1)}, u32[]{:S(2)}, u32[]{:S(2)}) collective-permute-start(bf16[272,256]{1,0:T(8,128)(2,1)S(1)} %collective-permute-done.2), channel_id=1, source_target_pairs={{24,16},{28,20},{0,24},{4,28},{25,17},{29,21},{1,25},{5,29},{26,18... | collective-permute-start | bytes 417800 | tf_op jit(solution)/shard_map/ppermute | solution.py:256
  32.7 8.1 %collective-permute-start.1 = (bf16[272,256]{1,0:T(8,128)(2,1)S(1)}, bf16[272,256]{1,0:T(8,128)(2,1)S(1)}, u32[]{:S(2)}, u32[]{:S(2)}) collective-permute-start(bf16[272,256]{1,0:T(8,128)(2,1)S(1)} %collective-permute-done.second_ref), channel_id=1, source_target_pairs={{8,12},{12,16},{16,20},{20,24},{24,28},{9,13},{13,17},{17,21},{21,... | collective-permute-start | bytes 417800 | tf_op jit(solution)/shard_map/ppermute | solution.py:251
